TPU v7x, 256 devices: a whole 4x4x8 slice. The times are simulated.
256 devices in a mesh: pair: 32 (over x, z), mom: 8 (over y, core).
Axes of the slice: x: 4, y: 4, z: 8, core: 2. Of those that a mesh axis runs over, the one named last changes fastest.
Arguments:
- peramb: bfloat16 [32, 768, 1536], P(None, 'pair'), may hold values from -0.21875 to 0.21875
- elementals: bfloat16 [16, 8, 2, 192, 384], P(None, 'mom'), may hold values from -0.4375 to 0.4375
- pair_times: int32 [32, 2], replicated, may hold values from 0 to 15
- pair_order: int32 [32], replicated, may hold values from 0 to 31, each once
- class_group: int32 [8], P('mom'), may hold values from 0 to 7
- gamma_columns: int32 [2, 4], replicated, may hold values from 0 to 3, each once within a row
- gamma_phases: int32 [2, 4], replicated, may hold values from 0 to 3
Outputs:
- correlator: float32 [2, 32, 8], P(None, 'pair')
Inputs may be any that keep to these rules, and one draw needn't show every extreme that they name: `pair_order`: each pair stands in exactly one slot. `gamma_columns`: each row is a permutation of the 4 spins.
All inputs are finite; a program needn't handle non-finite values.
Results may differ from a plain program's by a relative error of at most 0.0063.
Values may be sent and summed in bfloat16 or wider, within the bound.
A program may use at most 128 MiB of HBM per device.

v0:
```python
import jax
import jax.numpy as jnp
from jax import lax
from jax.sharding import PartitionSpec as P

GROUPS = 8


def phase_parts(phases):
    twist_real = (phases == 0).astype(jnp.float32) - (phases == 2).astype(jnp.float32)
    twist_imaginary = (phases == 1).astype(jnp.float32) - (phases == 3).astype(jnp.float32)
    return (twist_real, twist_imaginary)


def product_rows(left, right):
    return lax.dot_general(
        left, right, (((1,), (1,)), ((), ())), preferred_element_type=jnp.float32
    )


def product_columns(left, right):
    return lax.dot_general(
        left, right, (((0,), (0,)), ((), ())), preferred_element_type=jnp.float32
    )


def sink_side(block_real, block_imaginary, element, columns, twist_real, twist_imaginary):
    vectors = element.shape[0]
    full_width = block_real.shape[0]
    spin_count = full_width // vectors
    element_real = element[:, :vectors]
    element_imaginary = element[:, vectors:]
    moved_real = jnp.take(block_real.reshape(full_width, spin_count, vectors), columns, axis=1)
    moved_imaginary = jnp.take(
        block_imaginary.reshape(full_width, spin_count, vectors), columns, axis=1
    )
    factor_real = twist_real.astype(jnp.bfloat16)[None, :, None]
    factor_imaginary = twist_imaginary.astype(jnp.bfloat16)[None, :, None]
    turned_real = factor_real * moved_real - factor_imaginary * moved_imaginary
    turned_imaginary = factor_real * moved_imaginary + factor_imaginary * moved_real
    rows_real = turned_real.reshape(full_width * spin_count, vectors)
    rows_imaginary = turned_imaginary.reshape(full_width * spin_count, vectors)
    inner_real = product_rows(rows_real, element_real) - product_rows(
        rows_imaginary, element_imaginary
    )
    inner_imaginary = product_rows(rows_real, element_imaginary) + product_rows(
        rows_imaginary, element_real
    )
    return (
        inner_real.reshape(full_width, full_width).astype(jnp.bfloat16),
        inner_imaginary.reshape(full_width, full_width).astype(jnp.bfloat16),
    )


def source_side(block_real, block_imaginary, element, columns, twist_real, twist_imaginary):
    vectors = element.shape[0]
    full_width = block_real.shape[0]
    spin_count = full_width // vectors
    element_real = element[:, :vectors]
    element_imaginary = element[:, vectors:]
    moved_real = jnp.take(block_real.reshape(spin_count, vectors, full_width), columns, axis=0)
    moved_imaginary = jnp.take(
        block_imaginary.reshape(spin_count, vectors, full_width), columns, axis=0
    )
    chirality = 1.0 - 2.0 * (jnp.arange(spin_count) >= spin_count // 2).astype(jnp.float32)
    column_signs = jnp.repeat(chirality, vectors)
    row_signs = jnp.take(chirality, columns)
    weight_real = ((twist_real * row_signs)[:, None, None] * column_signs[None, None, :]).astype(
        jnp.bfloat16
    )
    weight_imaginary = (
        (twist_imaginary * row_signs)[:, None, None] * column_signs[None, None, :]
    ).astype(jnp.bfloat16)
    turned_real = weight_real * moved_real + weight_imaginary * moved_imaginary
    turned_imaginary = weight_imaginary * moved_real - weight_real * moved_imaginary
    final_real = jnp.einsum(
        "xj,bjs->bxs", element_real, turned_real, preferred_element_type=jnp.float32
    ) - jnp.einsum(
        "xj,bjs->bxs", element_imaginary, turned_imaginary, preferred_element_type=jnp.float32
    )
    final_imaginary = jnp.einsum(
        "xj,bjs->bxs", element_real, turned_imaginary, preferred_element_type=jnp.float32
    ) + jnp.einsum(
        "xj,bjs->bxs", element_imaginary, turned_real, preferred_element_type=jnp.float32
    )
    return (
        final_real.reshape(full_width, full_width).astype(jnp.bfloat16),
        final_imaginary.reshape(full_width, full_width).astype(jnp.bfloat16),
    )


def pair_value(block, sink_elements, source_elements, gamma_columns, sink_twist, source_twist):
    full_width = block.shape[0]
    block_real = block[:, :full_width]
    block_imaginary = block[:, full_width:]
    meson_real = []
    meson_imaginary = []
    for member in range(2):
        sink_real, sink_imaginary = sink_side(
            block_real,
            block_imaginary,
            sink_elements[0, member],
            gamma_columns[0],
            sink_twist[0],
            sink_twist[1],
        )
        source_real, source_imaginary = source_side(
            block_real,
            block_imaginary,
            source_elements[0, 1 - member],
            gamma_columns[1],
            source_twist[0],
            source_twist[1],
        )
        meson_real.append(
            product_columns(sink_real, source_real)
            - product_columns(sink_imaginary, source_imaginary)
        )
        meson_imaginary.append(
            product_columns(sink_real, source_imaginary)
            + product_columns(sink_imaginary, source_real)
        )
    first_real = jnp.trace(meson_real[0])
    first_imaginary = jnp.trace(meson_imaginary[0])
    second_real = jnp.trace(meson_real[1])
    second_imaginary = jnp.trace(meson_imaginary[1])
    direct_real = first_real * second_real - first_imaginary * second_imaginary
    direct_imaginary = first_real * second_imaginary + first_imaginary * second_real
    box_real = jnp.sum(meson_real[0] * meson_real[1].T) - jnp.sum(
        meson_imaginary[0] * meson_imaginary[1].T
    )
    box_imaginary = jnp.sum(meson_real[0] * meson_imaginary[1].T) + jnp.sum(
        meson_imaginary[0] * meson_real[1].T
    )
    values_real = [(direct_real - box_real) * 0.0625]
    values_imaginary = [(direct_imaginary - box_imaginary) * 0.0625]
    return (jnp.stack(values_real), jnp.stack(values_imaginary))


def per_device(
    peramb, elementals, pair_times, pair_order, class_group, gamma_columns, gamma_phases
):
    slots_device = pair_order.shape[0] // lax.axis_size("pair")
    ordered = jnp.take(peramb, pair_order, axis=0)
    blocks = lax.all_to_all(ordered, "pair", split_axis=0, concat_axis=1, tiled=True)
    sink_twist = phase_parts(gamma_phases[0])
    source_twist = phase_parts(gamma_phases[1])
    first_slot = lax.axis_index("pair") * slots_device
    chosen = lax.dynamic_index_in_dim(pair_order, first_slot + 0, 0, keepdims=False)
    times_here = lax.dynamic_index_in_dim(pair_times, chosen, 0, keepdims=False)
    sink_elements = lax.dynamic_index_in_dim(elementals, times_here[0], 0, keepdims=False)
    source_elements = lax.dynamic_index_in_dim(elementals, times_here[1], 0, keepdims=False)
    value_real, value_imaginary = pair_value(
        blocks[0], sink_elements, source_elements, gamma_columns, sink_twist, source_twist
    )
    rows_real = [value_real]
    rows_imaginary = [value_imaginary]
    values = jnp.stack([jnp.stack(rows_real), jnp.stack(rows_imaginary)])
    membership = (class_group[:, None] == jnp.arange(GROUPS, dtype=jnp.int32)[None, :]).astype(
        jnp.float32
    )
    partial_sums = jnp.sum(values[:, :, :, None] * membership[None, None, :, :], axis=2)
    return lax.psum(partial_sums, "mom")


def solution(mesh):
    placed = (P(None, "pair", None), P(None, "mom", None, None, None), P(), P(), P("mom"), P(), P())
    return jax.shard_map(
        per_device, mesh=mesh, in_specs=placed, out_specs=P(None, "pair", None), check_vma=False
    )
```

profile of v0, /device:TPU:1, one launch (start us, length us, event | category | flops | bytes accessed | tf_op | source)
XLA Modules:
  0.0 218.7 jit_solution(11591611471587458960)
XLA Ops:
  0.0 0.8 compare_select_fusion.2
  0.8 0.7 compare_and_fusion.2
  1.5 0.2 copy-done
  1.7 2.1 gather_fusion
  3.8 3.4 %broadcast_select_fusion = bf16[32,24,1536]{2,1,0:T(8,128)(2,1)} fusion(bf16[32,24,1536]{2,1,0:T(8,128)(2,1)} %gather_fusion, pred[32]{0:T(512)(128)(4,1)S(1)} %compare_and_fusion.2), kind=kLoop, calls=%fused_computation.31 | loop fusion | flops 1179648 | bytes 4718624 | tf_op jit(solution)/shard_map/jit(_take)/select_n | solution.py:144
  7.2 12.0 %all-to-all-start = ((bf16[32,24,1536]{2,1,0:T(8,128)(2,1)}), bf16[32,24,1536]{2,1,0:T(8,128)(2,1)S(1)}, u32[]{:S(2)}, u32[]{:S(2)}) async-start(bf16[32,24,1536]{2,1,0:T(8,128)(2,1)} %broadcast_select_fusion), calls=%async_computation | async-start | bytes 4718592 | tf_op jit(solution)/shard_map/all_to_all | solution.py:145
  19.2 0.6 dynamic_slice.15
  21.8 0.6 fusion.40
  25.0 0.6 gather_fusion.3
  27.7 1.1 dynamic-slice_bitcast_fusion
  29.0 44.6 %all-to-all-done = bf16[32,24,1536]{2,1,0:T(8,128)(2,1)S(1)} async-done(((bf16[32,24,1536]{2,1,0:T(8,128)(2,1)}), bf16[32,24,1536]{2,1,0:T(8,128)(2,1)S(1)}, u32[]{:S(2)}, u32[]{:S(2)}) %all-to-all-start) | async-done | bytes 2359328 | tf_op jit(solution)/shard_map/all_to_all | solution.py:145
  73.6 1.4 copy-done.7
  75.0 1.8 fusion.39
  76.8 1.4 copy.27
  78.2 1.4 copy.28
  79.7 2.9 %gather_fusion.1 = bf16[4,768,192]{1,2,0:T(8,128)(2,1)} fusion(bf16[768,4,192]{0,2,1:T(8,128)(2,1)} %bitcast.136, s32[1024]{0:T(1024)S(1)} %get-tuple-element.44), kind=kCustom, calls=%fused_computation.clone | custom fusion | bytes 2359312 | tf_op jit(solution)/shard_map/jit(_take)/gather | solution.py:33
  82.6 3.0 %gather_fusion.2 = bf16[4,768,192]{1,2,0:T(8,128)(2,1)} fusion(bf16[768,4,192]{0,2,1:T(8,128)(2,1)} %bitcast.135, s32[1024]{0:T(1024)S(1)} %get-tuple-element.44), kind=kCustom, calls=%fused_computation.3.clone | custom fusion | bytes 2359312 | tf_op jit(solution)/shard_map/jit(_take)/gather | solution.py:34
  85.6 3.0 %fusion.9 = (bf16[768,4,192]{0,2,1:T(8,128)(2,1)}, bf16[768,4,192]{0,2,1:T(8,128)(2,1)}) fusion(bf16[4]{0:T(256)(128)(2,1)S(1)} %get-tuple-element.37, bf16[4]{0:T(256)(128)(2,1)S(1)} %get-tuple-element.36, bf16[4,768,192]{1,2,0:T(8,128)(2,1)S(1)} %copy-done.10, pred[4]{0:T(512)(128)(4,1)S(1)} %get-tuple-element.34, bf16[4,768,192]{1,2,0:T(8,128)(2,1)} %gather_fusion.2), kind=kLoop, calls=%fused_computation.39 | loop fusion | flops 4718592 | bytes 4718612 | tf_op jit(solution)/shard_map/add | solution.py:40
  88.6 3.6 %copy.29 = bf16[768,4,192]{2,1,0:T(4,128)(2,1)} copy(bf16[768,4,192]{0,2,1:T(8,128)(2,1)} %get-tuple-element.21) | data formatting | bytes 2359296 | tf_op jit(solution)/shard_map/sub | solution.py:39
  92.3 2.7 %reshape.267 = bf16[3072,192]{1,0:T(8,128)(2,1)S(1)} reshape(bf16[768,4,192]{2,1,0:T(4,128)(2,1)} %copy.29) | data formatting | bytes 2359296 | tf_op jit(solution)/shard_map/reshape | solution.py:41
  95.0 2.1 fusion.14
  97.1 2.2 fusion.10
  99.3 2.1 fusion.20
  101.4 2.1 fusion.16
  103.5 1.9 gather_fusion.5
  105.4 1.7 gather_fusion.4
  107.1 1.7 multiply_subtract_fusion
  108.8 0.5 fusion.24
  109.2 1.9 fusion.25
  111.1 1.9 fusion.23
  113.0 1.9 fusion.22
  114.8 1.6 subtract_convert_fusion
  116.4 2.2 %copy.30 = bf16[768,4,192]{2,1,0:T(4,128)(2,1)} copy(bf16[768,4,192]{0,2,1:T(8,128)(2,1)S(1)} %copy-done.11) | data formatting | bytes 2359296 | tf_op jit(solution)/shard_map/add | solution.py:40
  118.6 2.7 %reshape.268 = bf16[3072,192]{1,0:T(8,128)(2,1)S(1)} reshape(bf16[768,4,192]{2,1,0:T(4,128)(2,1)} %copy.30) | data formatting | bytes 2359296 | tf_op jit(solution)/shard_map/reshape | solution.py:42
  121.4 3.4 %fusion.2 = bf16[3072,192]{0,1:T(8,128)(2,1)} fusion(f32[3072,192]{0,1:T(8,128)} %fusion.14, bf16[3072,192]{1,0:T(8,128)(2,1)S(1)} %reshape.268, bf16[192,384]{1,0:T(8,128)(2,1)S(1)} %get-tuple-element.46), kind=kOutput, calls=%fused_computation.12 | convolution fusion | flops 227672064 | bytes 5210112 | tf_op jit(solution)/shard_map/dot_general | solution.py:16
  124.7 2.6 %copy.34 = bf16[3072,192]{1,0:T(8,128)(2,1)} copy(bf16[3072,192]{0,1:T(8,128)(2,1)} %fusion.2) | data formatting | bytes 2359296 | tf_op jit(solution)/shard_map/convert_element_type | solution.py:50
  127.3 3.9 %convert_element_type.192 = bf16[768,768]{1,0:T(8,128)(2,1)} reshape(bf16[3072,192]{1,0:T(8,128)(2,1)} %copy.34) | data formatting | bytes 2359296 | tf_op jit(solution)/shard_map/convert_element_type | solution.py:50
  131.2 3.7 %add_convert_fusion = bf16[4,768,192]{1,2,0:T(8,128)(2,1)} fusion(f32[4,768,192]{1,2,0:T(8,128)} %fusion.25, bf16[4,192,768]{2,1,0:T(8,128)(2,1)} %copy-done.2, bf16[192,384]{1,0:T(8,128)(2,1)S(1)} %get-tuple-element.24), kind=kOutput, calls=%fused_computation.25 | convolution fusion | flops 227672064 | bytes 4816896 | tf_op jit(solution)/shard_map/xj,bjs->bxs/dot_general | solution.py:83
  135.0 1.7 fusion.3
  136.7 2.6 %copy.35 = bf16[3072,192]{1,0:T(8,128)(2,1)} copy(bf16[3072,192]{0,1:T(8,128)(2,1)} %fusion.3) | data formatting | bytes 2359296 | tf_op jit(solution)/shard_map/convert_element_type | solution.py:51
  139.3 3.9 %convert_element_type.197 = bf16[768,768]{1,0:T(8,128)(2,1)} reshape(bf16[3072,192]{1,0:T(8,128)(2,1)} %copy.35) | data formatting | bytes 2359296 | tf_op jit(solution)/shard_map/convert_element_type | solution.py:51
  143.2 2.9 %fusion.42 = f32[768,768]{0,1:T(8,128)S(1)} fusion(bf16[768,768]{1,0:T(8,128)(2,1)} %convert_element_type.192, bf16[768,768]{1,0:T(8,128)(2,1)} %bitcast.139), kind=kOutput, calls=%fused_computation.115 | convolution fusion | flops 905969664 | bytes 4718592 | tf_op jit(solution)/shard_map/dot_general | solution.py:22
  146.2 1.2 fusion.44
  147.4 3.3 %select_reduce_fusion.2 = (f32[]{:T(128)}, f32[768,768]{0,1:T(8,128)}) fusion(f32[768,768]{0,1:T(8,128)S(1)} %fusion.42, bf16[768,768]{1,0:T(8,128)(2,1)S(1)} %copy-done.19, bf16[768,768]{1,0:T(8,128)(2,1)S(1)} %bitcast.144), kind=kOutput, calls=%fused_computation.24 | convolution fusion | flops 908328960 | bytes 7077892 | tf_op jit(solution)/shard_map/dot_general | solution.py:22
  150.8 3.3 %select_reduce_fusion = (f32[]{:T(128)}, f32[768,768]{0,1:T(8,128)}) fusion(f32[768,768]{0,1:T(8,128)S(1)} %fusion.44, bf16[768,768]{1,0:T(8,128)(2,1)S(1)} %copy-done.19, bf16[768,768]{1,0:T(8,128)(2,1)S(1)} %bitcast.140), kind=kOutput, calls=%fused_computation.22 | convolution fusion | flops 908328960 | bytes 7077892 | tf_op jit(solution)/shard_map/dot_general | solution.py:22
  154.1 1.5 add_convert_fusion.1
  155.6 0.5 copy-done.4
  156.2 1.7 fusion
  157.9 2.5 %copy.31 = bf16[3072,192]{1,0:T(8,128)(2,1)} copy(bf16[3072,192]{0,1:T(8,128)(2,1)} %fusion) | data formatting | bytes 2359296 | tf_op jit(solution)/shard_map/convert_element_type | solution.py:50
  160.4 3.9 %convert_element_type.176 = bf16[768,768]{1,0:T(8,128)(2,1)} reshape(bf16[3072,192]{1,0:T(8,128)(2,1)} %copy.31) | data formatting | bytes 2359296 | tf_op jit(solution)/shard_map/convert_element_type | solution.py:50
  164.3 3.4 %fusion.1 = bf16[3072,192]{0,1:T(8,128)(2,1)} fusion(f32[3072,192]{0,1:T(8,128)} %fusion.16, bf16[3072,192]{1,0:T(8,128)(2,1)S(1)} %reshape.268, bf16[192,384]{1,0:T(8,128)(2,1)S(1)} %get-tuple-element.45), kind=kOutput, calls=%fused_computation.11 | convolution fusion | flops 227672064 | bytes 5210112 | tf_op jit(solution)/shard_map/dot_general | solution.py:16
  167.7 1.6 copy.32
  169.3 2.5 %convert_element_type.187 = bf16[768,768]{1,0:T(8,128)(2,1)} reshape(bf16[3072,192]{1,0:T(8,128)(2,1)S(1)} %copy.32) | data formatting | bytes 2359296 | tf_op jit(solution)/shard_map/convert_element_type | solution.py:51
  171.8 2.3 %subtract_convert_fusion.1 = bf16[4,768,192]{1,2,0:T(8,128)(2,1)S(1)} fusion(f32[4,768,192]{1,2,0:T(8,128)} %fusion.22, bf16[4,192,768]{2,1,0:T(8,128)(2,1)S(1)} %get-tuple-element.18, bf16[192,384]{1,0:T(8,128)(2,1)S(1)} %get-tuple-element.25), kind=kOutput, calls=%fused_computation.29 | convolution fusion | flops 227672064 | bytes 4816896 | tf_op jit(solution)/shard_map/xj,bjs->bxs/dot_general | solution.py:78
  174.1 2.5 %fusion.43 = f32[768,768]{1,0:T(8,128)} fusion(bf16[768,768]{1,0:T(8,128)(2,1)S(1)} %copy-done.17, bf16[768,768]{1,0:T(8,128)(2,1)S(1)} %bitcast.141), kind=kOutput, calls=%fused_computation.116 | convolution fusion | flops 905969664 | bytes 4718592 | tf_op jit(solution)/shard_map/dot_general | solution.py:22
  176.7 1.1 fusion.41
  177.8 0.1 copy-done.12
  178.0 1.2 convolution_subtract_fusion.3
  179.1 2.2 copy.33
  181.3 6.8 %fusion.4 = (f32[]{:T(128)}, f32[]{:T(128)}, f32[]{:T(128)}, f32[]{:T(128)}, f32[768,768]{1,0:T(8,128)}) fusion(f32[768,768]{0,1:T(8,128)} %get-tuple-element.39, f32[768,768]{1,0:T(8,128)S(1)} %convolution_subtract_fusion.3, f32[768,768]{0,1:T(8,128)} %get-tuple-element.41, f32[768,768]{1,0:T(8,128)} %fusion.43, bf16[768,768]{1,0:T(8,128)(2,1)S(1)} %copy-done.12, ...), kind=kOutput, calls=%fused_computation.16 | convolution fusion | flops 911278080 | bytes 14155792 | tf_op jit(solution)/shard_map/dot_general | solution.py:22
  188.1 3.1 %copy.38 = f32[768,768]{0,1:T(8,128)} copy(f32[768,768]{1,0:T(8,128)} %get-tuple-element.42) | data formatting | bytes 4718592 | tf_op jit(solution)/shard_map/add | solution.py:120
  191.2 2.5 %select_reduce_fusion.1 = f32[]{:T(128)} fusion(f32[768,768]{0,1:T(8,128)} %copy.38), kind=kLoop, calls=%fused_computation.23 | loop fusion | flops 1769471 | bytes 2359300 | tf_op jit(solution)/shard_map/jit(trace)/reduce_sum | solution.py:124
  193.7 0.7 select_reduce_fusion.3
  201.9 16.8 %psum.7 = f32[2,1,8]{2,1,0:T(1,128)} all-reduce(f32[2,1,8]{2,1,0:T(1,128)S(1)} %broadcast_multiply_fusion), channel_id=1, replica_groups=mesh['pair'=32,'mom'=8] {'mom'}, use_global_device_ids=true, to_apply=%region_8.12 | all-reduce | flops 16 | bytes 128 | tf_op jit(solution)/shard_map/psum | solution.py:163
  (58 shorter events, 0.7 us)
Async XLA Ops:
  0.0 1.7 copy-start
  7.2 12.0 %copy-start.23 = (s32[32]{0:T(128)S(1)}, s32[32]{0:T(128)}, u32[]{:S(2)}) copy-start(s32[32]{0:T(128)} %param.16) | copy-start | bytes 388
  7.2 14.6 %copy-start.21 = (s32[32,2]{0,1:T(2,128)S(1)}, s32[32,2]{0,1:T(2,128)}, u32[]{:S(2)}) copy-start(s32[32,2]{0,1:T(2,128)} %param.15) | copy-start | bytes 772
  7.2 17.8 %copy-start.20 = (s32[2,4]{1,0:T(2,128)S(1)}, s32[2,4]{1,0:T(2,128)}, u32[]{:S(2)}) copy-start(s32[2,4]{1,0:T(2,128)} %param.18) | copy-start | bytes 100
  7.2 66.4 %all-to-all-start = ((bf16[32,24,1536]{2,1,0:T(8,128)(2,1)}), bf16[32,24,1536]{2,1,0:T(8,128)(2,1)S(1)}, u32[]{:S(2)}, u32[]{:S(2)}) async-start(bf16[32,24,1536]{2,1,0:T(8,128)(2,1)} %broadcast_select_fusion), calls=%async_computation | async-start | bytes 4718592 | tf_op jit(solution)/shard_map/all_to_all | solution.py:145
  19.2 9.6 %copy-start.22 = (s32[2,4]{1,0:T(2,128)S(1)}, s32[2,4]{1,0:T(2,128)}, u32[]{:S(2)}) copy-start(s32[2,4]{1,0:T(2,128)} %param.19) | copy-start | bytes 100
  73.6 1.4 copy-start.7
  76.8 5.8 %copy-start.6 = (bf16[768,768]{1,0:T(8,128)(2,1)}, bf16[768,768]{1,0:T(8,128)(2,1)S(1)}, u32[]{:S(2)}) copy-start(bf16[768,768]{1,0:T(8,128)(2,1)S(1)} %get-tuple-element.22) | copy-start | bytes 3538948
  82.6 3.0 %copy-start.10 = (bf16[4,768,192]{1,2,0:T(8,128)(2,1)S(1)}, bf16[4,768,192]{1,2,0:T(8,128)(2,1)}, u32[]{:S(2)}) copy-start(bf16[4,768,192]{1,2,0:T(8,128)(2,1)} %gather_fusion.1) | copy-start | bytes 3538948
  108.7 4.2 %copy-start.2 = (bf16[4,192,768]{2,1,0:T(8,128)(2,1)}, bf16[4,192,768]{2,1,0:T(8,128)(2,1)S(1)}, u32[]{:S(2)}) copy-start(bf16[4,192,768]{2,1,0:T(8,128)(2,1)S(1)} %get-tuple-element.19) | copy-start | bytes 3538948
  114.8 1.6 copy-start.11
  131.2 3.7 %copy-start.5 = (f32[3072,192]{0,1:T(8,128)S(1)}, f32[3072,192]{0,1:T(8,128)}, u32[]{:S(2)}) copy-start(f32[3072,192]{0,1:T(8,128)} %fusion.10) | copy-start | bytes 7077892
  143.2 2.9 %copy-start.16 = (bf16[4,768,192]{1,2,0:T(8,128)(2,1)S(1)}, bf16[4,768,192]{1,2,0:T(8,128)(2,1)}, u32[]{:S(2)}) copy-start(bf16[4,768,192]{1,2,0:T(8,128)(2,1)} %add_convert_fusion) | copy-start | bytes 3538948
  143.2 2.9 %copy-start.18 = (bf16[768,768]{1,0:T(8,128)(2,1)S(1)}, bf16[768,768]{1,0:T(8,128)(2,1)}, u32[]{:S(2)}) copy-start(bf16[768,768]{1,0:T(8,128)(2,1)} %convert_element_type.192) | copy-start | bytes 3538948
  146.2 1.3 copy-start.19
  147.4 3.3 %copy-start.14 = (bf16[4,768,192]{1,2,0:T(8,128)(2,1)S(1)}, bf16[4,768,192]{1,2,0:T(8,128)(2,1)}, u32[]{:S(2)}) copy-start(bf16[4,768,192]{1,2,0:T(8,128)(2,1)} %subtract_convert_fusion) | copy-start | bytes 3538948
  150.7 3.3 %copy-start.3 = (bf16[4,192,768]{2,1,0:T(8,128)(2,1)S(1)}, bf16[4,192,768]{2,1,0:T(8,128)(2,1)}, u32[]{:S(2)}) copy-start(bf16[4,192,768]{2,1,0:T(8,128)(2,1)} %copy-done.2) | copy-start | bytes 3538948
  150.7 3.3 %copy-start.8 = (f32[4,768,192]{1,2,0:T(8,128)S(1)}, f32[4,768,192]{1,2,0:T(8,128)}, u32[]{:S(2)}) copy-start(f32[4,768,192]{1,2,0:T(8,128)} %fusion.23) | copy-start | bytes 7077892
  154.1 2.1 copy-start.4
  171.8 2.3 %copy-start.15 = (bf16[4,768,192]{1,2,0:T(8,128)(2,1)S(1)}, bf16[4,768,192]{1,2,0:T(8,128)(2,1)}, u32[]{:S(2)}) copy-start(bf16[4,768,192]{1,2,0:T(8,128)(2,1)} %add_convert_fusion.1) | copy-start | bytes 3538948
  171.8 2.3 %copy-start.17 = (bf16[768,768]{1,0:T(8,128)(2,1)S(1)}, bf16[768,768]{1,0:T(8,128)(2,1)}, u32[]{:S(2)}) copy-start(bf16[768,768]{1,0:T(8,128)(2,1)} %convert_element_type.176) | copy-start | bytes 3538948
  174.1 2.6 %copy-start.13 = (bf16[4,768,192]{1,2,0:T(8,128)(2,1)}, bf16[4,768,192]{1,2,0:T(8,128)(2,1)S(1)}, u32[]{:S(2)}) copy-start(bf16[4,768,192]{1,2,0:T(8,128)(2,1)S(1)} %subtract_convert_fusion.1) | copy-start | bytes 3538948
  176.7 1.3 copy-start.12
  191.2 2.5 %copy-start.9 = (f32[768,768]{0,1:T(8,128)S(1)}, f32[768,768]{0,1:T(8,128)}, u32[]{:S(2)}) copy-start(f32[768,768]{0,1:T(8,128)} %copy.33) | copy-start | bytes 7077892
  191.2 27.5 %copy-start.1 = (bf16[32,24,1536]{2,1,0:T(8,128)(2,1)S(1)}, bf16[32,24,1536]{2,1,0:T(8,128)(2,1)}, u32[]{:S(2)}) copy-start(bf16[32,24,1536]{2,1,0:T(8,128)(2,1)} %param.13) | copy-start | bytes 7077892
where the time goes:
time: 220 us; the launch traced here: 219 us
  local copies, waits for them, and re-layouts  62 us (28%)
  matrix products  56.3 us (26%)
  waiting for transfers between devices  44.6 us (20%)
  blocking collectives  16.8 us (8%)
  between operations  14 us (6%)
  other arithmetic  13 us (6%)
  starting transfers between devices  12 us (5%)
    all_to_all x1, waiting for transfers between devices, per_device(): lax.all_to_all(ordered, 'pair', split_axis=0, concat_axis=1, tiled=True)  44.6 us
    dot_general x8, matrix products, product_columns(): lax.dot_general(left, right, (((0,), (0,)), ((), ())), preferred_element_...  22.4 us
    dot_general x8, matrix products, product_rows(): lax.dot_general(left, right, (((1,), (1,)), ((), ())), preferred_element_...  18.7 us
    psum x1, blocking collectives, per_device(): return lax.psum(partial_sums, 'mom')  16.8 us
    convert_element_type x4, local copies, waits for them, and re-layouts, sink_side(): inner_real.reshape(full_width, full_width).astype(jnp.bfloat16)  12.9 us
    all_to_all x1, starting transfers between devices, per_device(): lax.all_to_all(ordered, 'pair', split_axis=0, concat_axis=1, tiled=True)  12 us
    convert_element_type x4, local copies, waits for them, and re-layouts, sink_side(): inner_imaginary.reshape(full_width, full_width).astype(jnp.bfloat16)  10.6 us
    dot_general x2, matrix products, source_side(): jnp.einsum('xj,bjs->bxs', element_imaginary, turned_real, preferred_eleme...  5.29 us
  transfers between devices with their start and end apart: 1, of which 1 were waited for; matrix products, arithmetic and copies ran while one was open for 2% of the time, Pallas kernels for 0%

commit v1 on v0

v1 whole, which is shorter than its diff:
```python
import functools

import jax
import jax.numpy as jnp
from jax import lax
from jax.experimental import pallas as pl
from jax.experimental.pallas import tpu as pltpu
from jax.sharding import PartitionSpec as P

MESH = pl.DeviceIdType.MESH
F32 = jnp.float32
BF16 = jnp.bfloat16

NX, NZ, NY = 4, 8, 4
GROUPS = 8
SPINS = 4
VECTORS = 192
FULL = SPINS * VECTORS
ROWS = 24
PIECE = 384
PEERS = 16
STEPS = 4
EACH = PEERS // STEPS


def place():
    pair = lax.axis_index("pair")
    mom = lax.axis_index("mom")
    return pair // NZ, pair % NZ, mom // 2, mom % 2


def plane(pair):
    return {"pair": pair, "mom": lax.axis_index("mom")}


def column(y, core):
    return {"pair": lax.axis_index("pair"), "mom": y * 2 + core}


def copy_to(src, dst, send, recv, device):
    return pltpu.make_async_remote_copy(
        src_ref=src, dst_ref=dst, send_sem=send, recv_sem=recv, device_id=device, device_id_type=MESH
    )


def exchange_kernel(
    order, peramb, out, staged, picked, load_sem, self_sem, send_plane, send_ring, recv_plane,
    recv_up, recv_down, recv_far, send_core, recv_core,
):
    x, z, y, core = place()
    up, down = (y + 1) % NY, (y + NY - 1) % NY
    far = (y + 2) % NY
    other = 1 - core
    columns = pl.ds(pl.multiple_of(y * PIECE, 128), PIECE)
    load = pltpu.make_async_copy(peramb.at[:, :, columns], staged, load_sem)
    load.start()

    def target(j):
        dx, dz = j // 4, 2 * (j % 4) + core
        return ((x + dx) % NX) * NZ + (z + dz) % NZ

    def source(j):
        dx, dz = j // 4, 2 * (j % 4) + core
        return ((x + NX - dx) % NX) * NZ + (z + NZ - dz) % NZ

    barrier = pltpu.get_barrier_semaphore()
    for j in range(1, PEERS):
        pl.semaphore_signal(barrier, inc=1, device_id=plane(source(j)), device_id_type=MESH)
    @pl.when(core == 1)
    def _():
        pl.semaphore_signal(barrier, inc=1, device_id=plane(source(0)), device_id_type=MESH)
    for device in (column(up, core), column(down, core), column(y, other)):
        pl.semaphore_signal(barrier, inc=1, device_id=device, device_id_type=MESH)
    load.wait()
    pl.semaphore_wait(barrier, PEERS - 1 + 3 + core)

    for j in range(PEERS):
        picked[j] = staged[order[target(j)]]
        group = j // EACH
        if j == 0:
            @pl.when(core == 0)
            def _():
                pltpu.make_async_copy(picked.at[j], out.at[y, core, j], self_sem).start()
            @pl.when(core == 1)
            def _():
                copy_to(picked.at[j], out.at[y, core, j], self_sem, recv_plane.at[STEPS], plane(target(j))).start()
        else:
            copy_to(
                picked.at[j], out.at[y, core, j], send_plane.at[group], recv_plane.at[group], plane(target(j))
            ).start()

    def block(piece, side, g):
        return out.at[piece, side, pl.ds(g * EACH, EACH)]

    def to_other(piece, kind, g):
        copy_to(
            block(piece, core, g), block(piece, core, g), send_core.at[kind, g], recv_core.at[kind, g],
            column(y, other),
        ).start()

    def to_ring(piece, where, send, recv, g):
        copy_to(block(piece, core, g), block(piece, core, g), send, recv, column(where, core)).start()

    def arrived(piece, side, sem, g):
        pltpu.make_async_copy(block(piece, side, g), block(piece, side, g), sem).wait()

    def own(g):
        if g == 0:
            few = out.at[y, core, pl.ds(1, EACH - 1)]
            pltpu.make_async_copy(few, few, recv_plane.at[g]).wait()
            one = out.at[y, core, 0]
            @pl.when(core == 0)
            def _():
                pltpu.make_async_copy(one, one, self_sem).wait()
            @pl.when(core == 1)
            def _():
                pltpu.make_async_copy(one, one, recv_plane.at[STEPS]).wait()
        else:
            arrived(y, core, recv_plane.at[g], g)
        to_ring(y, up, send_ring.at[0, g], recv_up.at[g], g)
        to_ring(y, down, send_ring.at[1, g], recv_down.at[g], g)
        to_other(y, 0, g)

    def near(g):
        arrived(down, core, recv_up.at[g], g)
        if g % 2 == 0:
            to_ring(down, up, send_ring.at[2, g], recv_far.at[g], g)
        to_other(down, 1, g)
        arrived(up, core, recv_down.at[g], g)
        if g % 2 == 1:
            to_ring(up, down, send_ring.at[2, g], recv_far.at[g], g)
        to_other(up, 2, g)

    def last(g):
        arrived(far, core, recv_far.at[g], g)
        to_other(far, 3, g)

    for g in range(STEPS + 2):
        if g < STEPS:
            own(g)
        if 0 <= g - 1 < STEPS:
            near(g - 1)
        if 0 <= g - 2 < STEPS:
            last(g - 2)
    for g in range(STEPS):
        for kind, piece in enumerate((y, down, up, far)):
            arrived(piece, other, recv_core.at[kind, g], g)
            arrived(piece, core, send_core.at[kind, g], g)
        for kind in range(3):
            arrived(y, core, send_ring.at[kind, g], g)
        few = picked.at[pl.ds(1, EACH - 1)] if g == 0 else picked.at[pl.ds(g * EACH, EACH)]
        pltpu.make_async_copy(few, few, send_plane.at[g]).wait()
    @pl.when(core == 1)
    def _():
        pltpu.make_async_copy(picked.at[0], picked.at[0], self_sem).wait()


def exchange(order, peramb):
    return pl.pallas_call(
        exchange_kernel,
        out_shape=jax.ShapeDtypeStruct((NY, 2, PEERS, ROWS, PIECE), BF16),
        in_specs=[pl.BlockSpec(memory_space=pltpu.SMEM), pl.BlockSpec(memory_space=pl.ANY)],
        out_specs=pl.BlockSpec(memory_space=pltpu.VMEM),
        scratch_shapes=[
            pltpu.VMEM((NX * NZ, ROWS, PIECE), BF16),
            pltpu.VMEM((PEERS, ROWS, PIECE), BF16),
            pltpu.SemaphoreType.DMA,
            pltpu.SemaphoreType.DMA,
            pltpu.SemaphoreType.DMA((STEPS,)),
            pltpu.SemaphoreType.DMA((3, STEPS)),
            pltpu.SemaphoreType.DMA((STEPS + 1,)),
            pltpu.SemaphoreType.DMA((STEPS,)),
            pltpu.SemaphoreType.DMA((STEPS,)),
            pltpu.SemaphoreType.DMA((STEPS,)),
            pltpu.SemaphoreType.DMA((4, STEPS)),
            pltpu.SemaphoreType.DMA((4, STEPS)),
        ],
        compiler_params=pltpu.CompilerParams(
            collective_id=0, has_side_effects=True, vmem_limit_bytes=32 * 1024 * 1024
        ),
        name="exchange",
    )(order, peramb)


def phase_parts(phase):
    real = jnp.where(phase == 0, 1.0, jnp.where(phase == 2, -1.0, 0.0)).astype(F32)
    imaginary = jnp.where(phase == 1, 1.0, jnp.where(phase == 3, -1.0, 0.0)).astype(F32)
    return real, imaginary


def spin_phases(columns, phases, side):
    found = []
    for spin in range(SPINS):
        real = jnp.float32(0.0)
        imaginary = jnp.float32(0.0)
        for row in range(SPINS):
            one, two = phase_parts(phases[side, row])
            chirality = 1.0 if (row if side == 0 else spin) < SPINS // 2 else -1.0
            here = jnp.where(columns[side, row] == spin, chirality, 0.0).astype(F32)
            real += here * one
            imaginary += here * two
        found.append((real, imaginary))
    return found


def padded_elements(tile):
    first = tile[:, :256].astype(F32)
    second = tile[:, 128:].astype(F32)
    lane = lax.broadcasted_iota(jnp.int32, first.shape, 1)
    real_low = jnp.where(lane < VECTORS, first, 0.0)
    imaginary_high = jnp.where(lane >= 64, second, 0.0)
    real_high = pltpu.roll(real_low, 64, 1)
    imaginary_low = pltpu.roll(imaginary_high, VECTORS, 1)
    return (real_low, imaginary_low), (real_high, imaginary_high)


def prepare_left(elements, columns, phases, side, left):
    turns = spin_phases(columns, phases, side)
    for member in range(2):
        padded = padded_elements(elements(member if side == 0 else 1 - member))
        for spin in range(SPINS):
            real, imaginary = padded[spin % 2]
            one, two = turns[spin]
            turned_real = one * real - two * imaginary
            turned_imaginary = one * imaginary + two * real
            base = member * 2 * VECTORS
            upper, lower = pl.ds(base, VECTORS), pl.ds(base + VECTORS, VECTORS)
            left[spin, 0, upper, :] = turned_real.astype(BF16)
            left[spin, 0, lower, :] = turned_imaginary.astype(BF16)
            if side == 0:
                left[spin, 1, upper, :] = (-turned_imaginary).astype(BF16)
                left[spin, 1, lower, :] = turned_real.astype(BF16)
            else:
                left[spin, 1, upper, :] = turned_imaginary.astype(BF16)
                left[spin, 1, lower, :] = (-turned_real).astype(BF16)


def gather_rows(pieces, block, x, z):
    def position(s):
        dx, dz = (x + NX - s // NZ) % NX, (z + NZ - s % NZ) % NZ
        return dz % 2, dx * 4 + dz // 2

    def step(i, carry):
        one, two = position(2 * i), position(2 * i + 1)
        for piece in range(NY):
            a = pieces[piece, one[0], one[1]].astype(F32)
            b = pieces[piece, two[0], two[1]].astype(F32)
            rows = pl.ds(pl.multiple_of(i * 2 * ROWS, 16), 2 * ROWS)
            block[rows, piece * PIECE:(piece + 1) * PIECE] = jnp.concatenate([a, b], axis=0).astype(BF16)
        return carry

    lax.fori_loop(0, NX * NZ // 2, step, 0)


def product(left, right, dims):
    return lax.dot_general(left, right, (dims, ((), ())), preferred_element_type=F32)


def sides(block, sink_left, source_left, sink, source):
    for spin in range(SPINS):
        start = (spin // 2) * PIECE + (spin % 2) * 128
        turned = product(sink_left[spin, 0], block[:, start:start + 256], ((1,), (1,)))
        turned += product(sink_left[spin, 1], block[:, FULL + start:FULL + start + 256], ((1,), (1,)))
        turned = turned.astype(BF16)
        for member in range(2):
            base = member * 2 * VECTORS
            sink[member, spin, :, :FULL] = turned[base:base + VECTORS]
            sink[member, spin, :, FULL:] = turned[base + VECTORS:base + 2 * VECTORS]
    for spin in range(SPINS):
        start = (spin // 2) * PIECE + (spin % 2) * 128
        turned = product(source_left[spin, 0], block[start:start + 256, :FULL], ((1,), (0,)))
        turned += product(source_left[spin, 1], block[start:start + 256, FULL:], ((1,), (0,)))
        for member in range(2):
            base = member * 2 * VECTORS
            real = turned[base:base + VECTORS]
            imaginary = turned[base + VECTORS:base + 2 * VECTORS]
            source[member, 0, spin, :, :FULL] = real.astype(BF16)
            source[member, 0, spin, :, FULL:] = imaginary.astype(BF16)
            source[member, 1, spin, :, :FULL] = (-imaginary).astype(BF16)
            source[member, 1, spin, :, FULL:] = real.astype(BF16)


def mesons(columns, sink, source, meson):
    width = 256
    for member in range(2):
        left = jnp.concatenate([sink[member, columns[0, spin]] for spin in range(SPINS)], axis=0)

        def step(n, carry):
            at = pl.ds(pl.multiple_of(n * width, 128), width)
            right = jnp.concatenate(
                [source[member, part, columns[1, spin], :, at] for part in range(2) for spin in range(SPINS)], axis=0
            )
            meson[member, :, at] = product(left, right, ((1,), (0,)))
            return carry

        lax.fori_loop(0, 2 * FULL // width, step, 0)


def slot_value(meson):
    tile = 128
    count = FULL // tile
    eye = (
        lax.broadcasted_iota(jnp.int32, (tile, tile), 0) == lax.broadcasted_iota(jnp.int32, (tile, tile), 1)
    ).astype(F32)
    traces = []
    for member in range(2):
        for part in range(2):
            total = jnp.zeros((tile, tile), F32)
            for i in range(count):
                total += eye * meson[member, i * tile:(i + 1) * tile, part * FULL + i * tile:part * FULL + (i + 1) * tile]
            traces.append(jnp.sum(total))

    def step(i, carry):
        box_real, box_imaginary = carry
        rows = pl.ds(pl.multiple_of(i * tile, tile), tile)
        for j in range(count):
            here = slice(j * tile, (j + 1) * tile)
            first_real = meson[0, rows, here]
            first_imaginary = meson[0, rows, FULL + j * tile:FULL + (j + 1) * tile]
            second_real = meson[1, here, rows].T
            second_imaginary = meson[1, here, pl.ds(pl.multiple_of(FULL + i * tile, tile), tile)].T
            box_real += first_real * second_real - first_imaginary * second_imaginary
            box_imaginary += first_real * second_imaginary + first_imaginary * second_real
        return box_real, box_imaginary

    zero = jnp.zeros((tile, tile), F32)
    box_real, box_imaginary = lax.fori_loop(0, count, step, (zero, zero))
    one_real, one_imaginary, two_real, two_imaginary = traces
    direct_real = one_real * two_real - one_imaginary * two_imaginary
    direct_imaginary = one_real * two_imaginary + one_imaginary * two_real
    return (direct_real - jnp.sum(box_real)) * 0.0625, (direct_imaginary - jnp.sum(box_imaginary)) * 0.0625


def contract_kernel(
    order, times, columns, phases, position, pieces, elements, value, block, sink_left, source_left, sink, source,
    meson, held, sems,
):
    x, z = position[0], position[1]
    chosen = order[position[0] * NZ + position[1]]
    loads = [pltpu.make_async_copy(elements.at[times[chosen, side], 0], held.at[side], sems.at[side]) for side in range(2)]
    for load in loads:
        load.start()
    gather_rows(pieces, block, x, z)
    for load in loads:
        load.wait()
    prepare_left(lambda member: held[0, member], columns, phases, 0, sink_left)
    prepare_left(lambda member: held[1, member], columns, phases, 1, source_left)
    sides(block, sink_left, source_left, sink, source)
    mesons(columns, sink, source, meson)
    real, imaginary = slot_value(meson)
    row = lax.broadcasted_iota(jnp.int32, (8, 128), 0)
    value[...] = jnp.where(row == 0, real, jnp.where(row == 1, imaginary, 0.0))


def contract(order, times, columns, phases, position, pieces, elements):
    smem = pl.BlockSpec(memory_space=pltpu.SMEM)
    return pl.pallas_call(
        contract_kernel,
        out_shape=jax.ShapeDtypeStruct((8, 128), F32),
        in_specs=[smem] * 5 + [pl.BlockSpec(memory_space=pltpu.VMEM), pl.BlockSpec(memory_space=pl.ANY)],
        out_specs=pl.BlockSpec(memory_space=pltpu.VMEM),
        scratch_shapes=[
            pltpu.VMEM((FULL, 2 * FULL), BF16),
            pltpu.VMEM((SPINS, 2, FULL, 256), BF16),
            pltpu.VMEM((SPINS, 2, FULL, 256), BF16),
            pltpu.VMEM((2, SPINS, VECTORS, 2 * FULL), BF16),
            pltpu.VMEM((2, 2, SPINS, VECTORS, 2 * FULL), BF16),
            pltpu.VMEM((2, FULL, 2 * FULL), F32),
            pltpu.VMEM((2, 2, VECTORS, 2 * VECTORS), BF16),
            pltpu.SemaphoreType.DMA((2,)),
        ],
        compiler_params=pltpu.CompilerParams(vmem_limit_bytes=56 * 1024 * 1024),
        name="contract",
    )(order, times, columns, phases, position, pieces, elements)


def per_device(peramb, elementals, pair_times, pair_order, class_group, gamma_columns, gamma_phases):
    pieces = exchange(pair_order, peramb)
    pair = lax.axis_index("pair")
    position = jnp.stack([pair // NZ, pair % NZ]).astype(jnp.int32)
    value = contract(pair_order, pair_times, gamma_columns, gamma_phases, position, pieces, elementals)
    membership = (class_group[0] == jnp.arange(GROUPS, dtype=jnp.int32)).astype(F32)
    partial = value[:2, :1, None].reshape(2, 1, 1) * membership[None, None, :]
    return lax.psum(partial, "mom")


def solution(mesh):
    placed = (P(None, "pair", None), P(None, "mom", None, None, None), P(), P(), P("mom"), P(), P())
    return jax.shard_map(
        per_device, mesh=mesh, in_specs=placed, out_specs=P(None, "pair", None), check_vma=False
    )
```

time: 220 us -> 74.8 us (0.34)
  the two profiles are of different devices: /device:TPU:1 before, /device:TPU:32 now
where the time goes in v1:
time: 74.8 us; the launch traced here: 74.6 us
  Pallas kernels  52.6 us (70%)
  blocking collectives  15.3 us (20%)
  local copies, waits for them, and re-layouts  5.2 us (7%)
    pallas_call x1, Pallas kernels, exchange(): pl.pallas_call(exchange_kernel, out_shape=jax.ShapeDtypeStruct((NY, 2, PE...  32.5 us
    pallas_call x1, Pallas kernels, contract(): pl.pallas_call(contract_kernel, out_shape=jax.ShapeDtypeStruct((8, 128),...  20.1 us
    psum x1, blocking collectives, per_device(): return lax.psum(partial, 'mom')  15.3 us
    unnamed x9, local copies, waits for them, and re-layouts  4.41 us

profile of v1, /device:TPU:32, one launch (start us, length us, event | category | flops | bytes accessed | tf_op | source)
XLA Modules:
  0.0 74.6 jit_solution(8179473337626214331)
XLA Ops:
  0.0 0.7 pad_add_fusion.position
  0.7 0.0 copy-start.1
  0.7 1.7 %copy-done.1 = bf16[32,24,1536]{2,1,0:T(8,128)(2,1)S(1)} copy-done((bf16[32,24,1536]{2,1,0:T(8,128)(2,1)S(1)}, bf16[32,24,1536]{2,1,0:T(8,128)(2,1)}, u32[]{:S(2)}) %copy-start.1) | copy-done | bytes 2359320
  2.3 0.0 copy-start.2
  2.3 0.7 copy-done.2
  3.0 0.0 copy-start.3
  3.0 32.5 %exchange.1.pieces = bf16[4,2,16,24,384]{4,3,2,1,0:T(8,128)(2,1)S(1)} custom-call(s32[32]{0:T(128)S(1)} %copy-done.2, bf16[32,24,1536]{2,1,0:T(8,128)(2,1)S(1)} %copy-done.1), custom_call_target="tpu_custom_call" | custom-call | tf_op jit(solution)/shard_map/exchange/pallas_call | solution.py:159
  35.5 0.0 copy-start
  35.5 1.4 %copy-done = bf16[4,2,16,24,384]{4,3,2,1,0:T(8,128)(2,1)} copy-done((bf16[4,2,16,24,384]{4,3,2,1,0:T(8,128)(2,1)}, bf16[4,2,16,24,384]{4,3,2,1,0:T(8,128)(2,1)S(1)}, u32[]{:S(2)}) %copy-start) | copy-done | bytes 2359320
  36.9 0.0 copy-done.3
  36.9 0.7 copy.9.times
  37.6 20.1 %contract.1 = f32[8,128]{1,0:T(8,128)} custom-call(s32[32]{0:T(128)} %order.3, s32[32,2]{1,0:T(8,128)} %copy.9.times, s32[2,4]{1,0:T(2,128)} %columns.1, s32[2,4]{1,0:T(2,128)} %phases.1, s32[2]{0:T(128)} %pad_add_fusion.position, bf16[4,2,16,24,384]{4,3,2,1,0:T(8,128)(2,1)} %copy-done, bf16[16,1,2,192,384]{4,3,2,1,0:T(8,128)(2,1)} %elements.1), custom_call_target="tpu_custom_call" | custom-call | tf_op jit(solution)/shard_map/contract/pallas_call | solution.py:357
  57.7 0.8 %slice_reduce_fusion = f32[2]{0:T(128)S(1)} fusion(f32[8,128]{1,0:T(8,128)} %contract.1), kind=kLoop, calls=%fused_computation.1 | loop fusion | bytes 16 | tf_op jit(solution)/shard_map/slice | solution.py:383
  59.2 0.1 broadcast_multiply_fusion
  59.3 15.3 %psum.7 = f32[2,1,8]{2,1,0:T(1,128)} all-reduce(f32[2,1,8]{2,1,0:T(1,128)S(1)} %broadcast_multiply_fusion), channel_id=1, replica_groups=mesh['pair'=32,'mom'=8] {'mom'}, use_global_device_ids=true, to_apply=%region_0.1 | all-reduce | flops 16 | bytes 128 | tf_op jit(solution)/shard_map/psum | solution.py:384
  (1 shorter events, 0.0 us)
Async XLA Ops:
  0.7 1.7 %copy-start.1 = (bf16[32,24,1536]{2,1,0:T(8,128)(2,1)S(1)}, bf16[32,24,1536]{2,1,0:T(8,128)(2,1)}, u32[]{:S(2)}) copy-start(bf16[32,24,1536]{2,1,0:T(8,128)(2,1)} %peramb.1) | copy-start | bytes 7077892
  2.3 0.7 copy-start.2
  3.0 33.9 %copy-start.3 = (s32[32,2]{0,1:T(2,128)S(1)}, s32[32,2]{0,1:T(2,128)}, u32[]{:S(2)}) copy-start(s32[32,2]{0,1:T(2,128)} %param.9) | copy-start | bytes 772
  35.5 1.4 %copy-start = (bf16[4,2,16,24,384]{4,3,2,1,0:T(8,128)(2,1)}, bf16[4,2,16,24,384]{4,3,2,1,0:T(8,128)(2,1)S(1)}, u32[]{:S(2)}) copy-start(bf16[4,2,16,24,384]{4,3,2,1,0:T(8,128)(2,1)S(1)} %exchange.1.pieces) | copy-start | bytes 7077892

commit v2 on v1

v2 whole, which is shorter than its diff:
```python
import jax
import jax.numpy as jnp
from jax import lax
from jax.experimental import pallas as pl
from jax.experimental.pallas import tpu as pltpu
from jax.sharding import PartitionSpec as P

MESH = pl.DeviceIdType.MESH
F32 = jnp.float32
BF16 = jnp.bfloat16

NX, NZ, NY = 4, 8, 4
GROUPS = 8
SPINS = 4
VECTORS = 192
FULL = SPINS * VECTORS
ROWS = 24
PIECE = 384
PEERS = 16


def place():
    pair = lax.axis_index("pair")
    mom = lax.axis_index("mom")
    return pair // NZ, pair % NZ, mom // 2, mom % 2


def plane(pair):
    return {"pair": pair, "mom": lax.axis_index("mom")}


def column(y, core):
    return {"pair": lax.axis_index("pair"), "mom": y * 2 + core}


def copy_to(src, dst, send, recv, device):
    return pltpu.make_async_remote_copy(
        src_ref=src, dst_ref=dst, send_sem=send, recv_sem=recv, device_id=device, device_id_type=MESH
    )


def phase_parts(phase):
    real = jnp.where(phase == 0, 1.0, jnp.where(phase == 2, -1.0, 0.0)).astype(F32)
    imaginary = jnp.where(phase == 1, 1.0, jnp.where(phase == 3, -1.0, 0.0)).astype(F32)
    return real, imaginary


def spin_phases(columns, phases, side):
    found = []
    for spin in range(SPINS):
        real = jnp.float32(0.0)
        imaginary = jnp.float32(0.0)
        for row in range(SPINS):
            one, two = phase_parts(phases[side, row])
            chirality = 1.0 if (row if side == 0 else spin) < SPINS // 2 else -1.0
            here = jnp.where(columns[side, row] == spin, chirality, 0.0).astype(F32)
            real += here * one
            imaginary += here * two
        found.append((real, imaginary))
    return found


def padded_elements(tile):
    first = tile[:, :256].astype(F32)
    second = tile[:, 128:].astype(F32)
    lane = lax.broadcasted_iota(jnp.int32, first.shape, 1)
    real_low = jnp.where(lane < VECTORS, first, 0.0)
    imaginary_high = jnp.where(lane >= 64, second, 0.0)
    real_high = pltpu.roll(real_low, 64, 1)
    imaginary_low = pltpu.roll(imaginary_high, VECTORS, 1)
    return (real_low, imaginary_low), (real_high, imaginary_high)


def prepare_left(elements, columns, phases, side, left):
    turns = spin_phases(columns, phases, side)
    for member in range(2):
        padded = padded_elements(elements(member if side == 0 else 1 - member))
        for spin in range(SPINS):
            real, imaginary = padded[spin % 2]
            one, two = turns[spin]
            turned_real = one * real - two * imaginary
            turned_imaginary = one * imaginary + two * real
            base = member * 2 * VECTORS
            upper, lower = pl.ds(base, VECTORS), pl.ds(base + VECTORS, VECTORS)
            left[spin, 0, upper, :] = turned_real.astype(BF16)
            left[spin, 0, lower, :] = turned_imaginary.astype(BF16)
            if side == 0:
                left[spin, 1, upper, :] = (-turned_imaginary).astype(BF16)
                left[spin, 1, lower, :] = turned_real.astype(BF16)
            else:
                left[spin, 1, upper, :] = turned_imaginary.astype(BF16)
                left[spin, 1, lower, :] = (-turned_real).astype(BF16)


def gather_rows(pieces, block, x, z):
    def position(s):
        dx, dz = (x + NX - s // NZ) % NX, (z + NZ - s % NZ) % NZ
        return dz % 2, dx * 4 + dz // 2

    def step(i, carry):
        one, two = position(2 * i), position(2 * i + 1)
        for piece in range(NY):
            a = pieces[piece, one[0], one[1]].astype(F32)
            b = pieces[piece, two[0], two[1]].astype(F32)
            rows = pl.ds(pl.multiple_of(i * 2 * ROWS, 16), 2 * ROWS)
            block[rows, piece * PIECE:(piece + 1) * PIECE] = jnp.concatenate([a, b], axis=0).astype(BF16)
        return carry

    lax.fori_loop(0, NX * NZ // 2, step, 0)


def product(left, right, dims):
    return lax.dot_general(left, right, (dims, ((), ())), preferred_element_type=F32)


def sides(block, sink_left, source_left, sink, source):
    for spin in range(SPINS):
        start = (spin // 2) * PIECE + (spin % 2) * 128
        turned = product(sink_left[spin, 0], block[:, start:start + 256], ((1,), (1,)))
        turned += product(sink_left[spin, 1], block[:, FULL + start:FULL + start + 256], ((1,), (1,)))
        turned = turned.astype(BF16)
        for member in range(2):
            base = member * 2 * VECTORS
            sink[member, spin, :, :FULL] = turned[base:base + VECTORS]
            sink[member, spin, :, FULL:] = turned[base + VECTORS:base + 2 * VECTORS]
    for spin in range(SPINS):
        start = (spin // 2) * PIECE + (spin % 2) * 128
        turned = product(source_left[spin, 0], block[start:start + 256, :FULL], ((1,), (0,)))
        turned += product(source_left[spin, 1], block[start:start + 256, FULL:], ((1,), (0,)))
        for member in range(2):
            base = member * 2 * VECTORS
            real = turned[base:base + VECTORS]
            imaginary = turned[base + VECTORS:base + 2 * VECTORS]
            source[member, 0, spin, :, :FULL] = real.astype(BF16)
            source[member, 0, spin, :, FULL:] = imaginary.astype(BF16)
            source[member, 1, spin, :, :FULL] = (-imaginary).astype(BF16)
            source[member, 1, spin, :, FULL:] = real.astype(BF16)


def mesons(columns, sink, source, meson):
    width = 256
    for member in range(2):
        left = jnp.concatenate([sink[member, columns[0, spin]] for spin in range(SPINS)], axis=0)

        def step(n, carry):
            at = pl.ds(pl.multiple_of(n * width, 128), width)
            right = jnp.concatenate(
                [source[member, part, columns[1, spin], :, at] for part in range(2) for spin in range(SPINS)], axis=0
            )
            meson[member, :, at] = product(left, right, ((1,), (0,)))
            return carry

        lax.fori_loop(0, 2 * FULL // width, step, 0)


def slot_value(meson):
    tile = 128
    count = FULL // tile
    eye = (
        lax.broadcasted_iota(jnp.int32, (tile, tile), 0) == lax.broadcasted_iota(jnp.int32, (tile, tile), 1)
    ).astype(F32)
    traces = []
    for member in range(2):
        for part in range(2):
            total = jnp.zeros((tile, tile), F32)
            for i in range(count):
                total += eye * meson[member, i * tile:(i + 1) * tile, part * FULL + i * tile:part * FULL + (i + 1) * tile]
            traces.append(jnp.sum(total))

    def step(i, carry):
        box_real, box_imaginary = carry
        rows = pl.ds(pl.multiple_of(i * tile, tile), tile)
        for j in range(count):
            here = slice(j * tile, (j + 1) * tile)
            first_real = meson[0, rows, here]
            first_imaginary = meson[0, rows, FULL + j * tile:FULL + (j + 1) * tile]
            second_real = meson[1, here, rows].T
            second_imaginary = meson[1, here, pl.ds(pl.multiple_of(FULL + i * tile, tile), tile)].T
            box_real += first_real * second_real - first_imaginary * second_imaginary
            box_imaginary += first_real * second_imaginary + first_imaginary * second_real
        return box_real, box_imaginary

    zero = jnp.zeros((tile, tile), F32)
    box_real, box_imaginary = lax.fori_loop(0, count, step, (zero, zero))
    one_real, one_imaginary, two_real, two_imaginary = traces
    direct_real = one_real * two_real - one_imaginary * two_imaginary
    direct_imaginary = one_real * two_imaginary + one_imaginary * two_real
    return (direct_real - jnp.sum(box_real)) * 0.0625, (direct_imaginary - jnp.sum(box_imaginary)) * 0.0625


def correlator_kernel(
    order, times, columns, phases, group, peramb, elementals, out, staged_own, staged_far, picked, pieces, held, block,
    sink_left, source_left, sink, source, meson, votes, load_sem, self_sem, send_plane, recv_plane, send_ring,
    recv_ring, send_core, recv_core, send_vote, recv_vote,
):
    x, z, y, core = place()
    mom = lax.axis_index("mom")
    up, down, far = (y + 1) % NY, (y + NY - 1) % NY, (y + 2) % NY
    other = 1 - core

    def target(j):
        dx, dz = j // 4, 2 * (j % 4) + core
        return ((x + dx) % NX) * NZ + (z + dz) % NZ

    def source_of(j):
        dx, dz = j // 4, 2 * (j % 4) + core
        return ((x + NX - dx) % NX) * NZ + (z + NZ - dz) % NZ

    def peer(step):
        return {"pair": lax.axis_index("pair"), "mom": (mom + step) % (2 * NY)}

    staged = (staged_own, staged_far)
    loads = []
    for phase, piece in enumerate((y, far)):
        at = pl.ds(pl.multiple_of(piece * PIECE, 128), PIECE)
        loads.append(pltpu.make_async_copy(peramb.at[:, :, at], staged[phase], load_sem.at[phase]))
    loads.append(pltpu.make_async_copy(elementals, held, load_sem.at[2]))
    for load in loads:
        load.start()

    barrier = pltpu.get_barrier_semaphore()
    for j in range(1, PEERS):
        pl.semaphore_signal(barrier, inc=1, device_id=plane(source_of(j)), device_id_type=MESH)
    @pl.when(core == 1)
    def _():
        pl.semaphore_signal(barrier, inc=1, device_id=plane(source_of(0)), device_id_type=MESH)
    for step in range(1, 2 * NY):
        pl.semaphore_signal(barrier, inc=1, device_id=peer(step), device_id_type=MESH)
    loads[0].wait()
    pl.semaphore_wait(barrier, PEERS - 1 + 2 * NY - 1 + core)

    def pick(phase):
        for j in range(PEERS):
            picked[phase, j] = staged[phase][order[target(j)]]

    def send_in_plane(phase, piece):
        for j in range(PEERS):
            src, dst = picked.at[phase, j], pieces.at[piece, core, j]
            if j == 0:
                @pl.when(core == 0)
                def _():
                    pltpu.make_async_copy(src, dst, recv_plane.at[phase]).start()
                @pl.when(core == 1)
                def _():
                    copy_to(src, dst, self_sem.at[phase], recv_plane.at[phase], plane(target(j))).start()
            else:
                copy_to(src, dst, send_plane.at[phase], recv_plane.at[phase], plane(target(j))).start()

    def sent_in_plane(phase):
        most = picked.at[phase, pl.ds(1, PEERS - 1)]
        pltpu.make_async_copy(most, most, send_plane.at[phase]).wait()
        @pl.when(core == 1)
        def _():
            one = picked.at[phase, 0]
            pltpu.make_async_copy(one, one, self_sem.at[phase]).wait()

    def finish(piece, side, sem):
        part = pieces.at[piece, side]
        pltpu.make_async_copy(part, part, sem).wait()

    def to_ring(way, where):
        part = pieces.at[y, core]
        copy_to(part, part, send_ring.at[way], recv_ring.at[way], column(where, core)).start()

    def to_other(kind, piece):
        part = pieces.at[piece, core]
        copy_to(part, part, send_core.at[kind], recv_core.at[kind], column(y, other)).start()

    pick(0)
    send_in_plane(0, y)
    loads[1].wait()
    pick(1)
    loads[2].wait()
    chosen = order[lax.axis_index("pair")]
    prepare_left(lambda member: held[times[0, chosen], 0, member], columns, phases, 0, sink_left)
    prepare_left(lambda member: held[times[1, chosen], 0, member], columns, phases, 1, source_left)

    finish(y, core, recv_plane.at[0])
    to_ring(0, up)
    to_ring(1, down)
    send_in_plane(1, far)
    to_other(0, y)
    finish(y, other, recv_core.at[0])
    finish(down, core, recv_ring.at[0])
    to_other(1, down)
    finish(up, core, recv_ring.at[1])
    to_other(2, up)
    finish(far, core, recv_plane.at[1])
    to_other(3, far)
    finish(down, other, recv_core.at[1])
    finish(up, other, recv_core.at[2])
    finish(far, other, recv_core.at[3])

    gather_rows(pieces, block, x, z)
    sides(block, sink_left, source_left, sink, source)
    mesons(columns, sink, source, meson)
    real, imaginary = slot_value(meson)

    row = lax.broadcasted_iota(jnp.int32, (8, 128), 0)
    lane = lax.broadcasted_iota(jnp.int32, (8, 128), 1)
    both = jnp.where(row == 0, real, jnp.where(row == 1, imaginary, 0.0))
    votes[mom] = jnp.where(lane == group[0], both, 0.0)
    for step in range(1, 2 * NY):
        copy_to(votes.at[mom], votes.at[mom], send_vote.at[step], recv_vote.at[step], peer(step)).start()

    sent_in_plane(0)
    sent_in_plane(1)
    for way in range(2):
        finish(y, core, send_ring.at[way])
    for kind, piece in enumerate((y, down, up, far)):
        finish(piece, core, send_core.at[kind])
    for step in range(1, 2 * NY):
        sender = (mom + 2 * NY - step) % (2 * NY)
        pltpu.make_async_copy(votes.at[sender], votes.at[sender], recv_vote.at[step]).wait()
    total = votes[0]
    for each in range(1, 2 * NY):
        total = total + votes[each]
    out[0] = total[0:1, :GROUPS]
    out[1] = total[1:2, :GROUPS]
    for step in range(1, 2 * NY):
        pltpu.make_async_copy(votes.at[mom], votes.at[mom], send_vote.at[step]).wait()


def per_device(peramb, elementals, pair_times, pair_order, class_group, gamma_columns, gamma_phases):
    smem = pl.BlockSpec(memory_space=pltpu.SMEM)
    anywhere = pl.BlockSpec(memory_space=pl.ANY)
    dma = pltpu.SemaphoreType.DMA
    return pl.pallas_call(
        correlator_kernel,
        out_shape=jax.ShapeDtypeStruct((2, 1, GROUPS), F32),
        in_specs=[smem] * 5 + [anywhere] * 2,
        out_specs=pl.BlockSpec(memory_space=pltpu.VMEM),
        scratch_shapes=[
            pltpu.VMEM((NX * NZ, ROWS, PIECE), BF16),
            pltpu.VMEM((NX * NZ, ROWS, PIECE), BF16),
            pltpu.VMEM((2, PEERS, ROWS, PIECE), BF16),
            pltpu.VMEM((NY, 2, PEERS, ROWS, PIECE), BF16),
            pltpu.VMEM(elementals.shape, BF16),
            pltpu.VMEM((FULL, 2 * FULL), BF16),
            pltpu.VMEM((SPINS, 2, FULL, 256), BF16),
            pltpu.VMEM((SPINS, 2, FULL, 256), BF16),
            pltpu.VMEM((2, SPINS, VECTORS, 2 * FULL), BF16),
            pltpu.VMEM((2, 2, SPINS, VECTORS, 2 * FULL), BF16),
            pltpu.VMEM((2, FULL, 2 * FULL), F32),
            pltpu.VMEM((2 * NY, 8, 128), F32),
            dma((3,)),
            dma((2,)),
            dma((2,)),
            dma((2,)),
            dma((2,)),
            dma((2,)),
            dma((4,)),
            dma((4,)),
            dma((2 * NY,)),
            dma((2 * NY,)),
        ],
        compiler_params=pltpu.CompilerParams(
            collective_id=0, has_side_effects=True, vmem_limit_bytes=60 * 1024 * 1024
        ),
        cost_estimate=pl.CostEstimate(flops=11_000_000_000, bytes_accessed=8_000_000, transcendentals=0),
        name="correlator",
    )(pair_order, pair_times.T, gamma_columns, gamma_phases, class_group, peramb, elementals)


def solution(mesh):
    placed = (P(None, "pair", None), P(None, "mom", None, None, None), P(), P(), P("mom"), P(), P())
    return jax.shard_map(
        per_device, mesh=mesh, in_specs=placed, out_specs=P(None, "pair", None), check_vma=False
    )
```

time: 74.8 us -> 55.3 us (0.74)
  the two profiles are of different devices: /device:TPU:32 before, /device:TPU:1 now
where the time goes in v2:
time: 55.3 us; the launch traced here: 55.2 us
  Pallas kernels  53.3 us (96%)
  local copies, waits for them, and re-layouts  1.24 us (2%)
  between operations  0.66 us (1%)
    pallas_call x1, Pallas kernels, per_device(): pl.pallas_call(correlator_kernel, out_shape=jax.ShapeDtypeStruct((2, 1, G...  53.3 us
    unnamed x1, local copies, waits for them, and re-layouts  1.24 us

profile of v2, /device:TPU:1, one launch (start us, length us, event | category | flops | bytes accessed | tf_op | source)
XLA Modules:
  0.0 55.2 jit_solution(12987214524154761862)
XLA Ops:
  0.7 53.3 %correlator.1 = f32[2,1,8]{2,1,0:T(1,128)} custom-call(s32[32]{0:T(128)} %order.1, s32[2,32]{1,0:T(2,128)} %bitcast.1, s32[2,4]{1,0:T(2,128)} %columns.1, s32[2,4]{1,0:T(2,128)} %phases.1, s32[1]{0:T(128)S(6)} %copy.9.group, bf16[32,24,1536]{2,1,0:T(8,128)(2,1)} %peramb.1, bf16[16,1,2,192,384]{4,3,2,1,0:T(8,128)(2,1)} %elementals.1), custom_call_target="tpu_custom_call" | custom-call | flops 11000000512 | bytes 8000000 | tf_op jit(solution)/shard_map/correlator/pallas_call | solution.py:328
  53.9 1.2 %copy.10 = f32[2,1,8]{2,1,0:T(1,128)} copy(f32[2,1,8]{2,1,0:T(1,128)} %correlator.1) | data formatting | bytes 128

commit v3 on v2

--- a/solution.py
+++ b/solution.py
@@ -113,76 +113,78 @@
     return lax.dot_general(left, right, (dims, ((), ())), preferred_element_type=F32)
 
 
+def triple(real, imaginary, sign):
+    real, imaginary = real.astype(BF16), imaginary.astype(BF16)
+    one, two = real.astype(F32), imaginary.astype(F32)
+    return real, imaginary, (one + two).astype(BF16), None if sign == 0 else (two - one).astype(BF16)
+
+
 def sides(block, sink_left, source_left, sink, source):
     for spin in range(SPINS):
         start = (spin // 2) * PIECE + (spin % 2) * 128
         turned = product(sink_left[spin, 0], block[:, start:start + 256], ((1,), (1,)))
         turned += product(sink_left[spin, 1], block[:, FULL + start:FULL + start + 256], ((1,), (1,)))
-        turned = turned.astype(BF16)
         for member in range(2):
             base = member * 2 * VECTORS
-            sink[member, spin, :, :FULL] = turned[base:base + VECTORS]
-            sink[member, spin, :, FULL:] = turned[base + VECTORS:base + 2 * VECTORS]
+            real, imaginary, both, _ = triple(turned[base:base + VECTORS], turned[base + VECTORS:base + 2 * VECTORS], 0)
+            sink[member, spin, :, :FULL] = both
+            sink[member, spin, :, FULL:2 * FULL] = real
+            sink[member, spin, :, 2 * FULL:] = imaginary
     for spin in range(SPINS):
         start = (spin // 2) * PIECE + (spin % 2) * 128
         turned = product(source_left[spin, 0], block[start:start + 256, :FULL], ((1,), (0,)))
         turned += product(source_left[spin, 1], block[start:start + 256, FULL:], ((1,), (0,)))
         for member in range(2):
             base = member * 2 * VECTORS
-            real = turned[base:base + VECTORS]
-            imaginary = turned[base + VECTORS:base + 2 * VECTORS]
-            source[member, 0, spin, :, :FULL] = real.astype(BF16)
-            source[member, 0, spin, :, FULL:] = imaginary.astype(BF16)
-            source[member, 1, spin, :, :FULL] = (-imaginary).astype(BF16)
-            source[member, 1, spin, :, FULL:] = real.astype(BF16)
-
-
-def mesons(columns, sink, source, meson):
-    width = 256
-    for member in range(2):
-        left = jnp.concatenate([sink[member, columns[0, spin]] for spin in range(SPINS)], axis=0)
-
-        def step(n, carry):
-            at = pl.ds(pl.multiple_of(n * width, 128), width)
-            right = jnp.concatenate(
-                [source[member, part, columns[1, spin], :, at] for part in range(2) for spin in range(SPINS)], axis=0
-            )
-            meson[member, :, at] = product(left, right, ((1,), (0,)))
-            return carry
-
-        lax.fori_loop(0, 2 * FULL // width, step, 0)
-
-
-def slot_value(meson):
-    tile = 128
-    count = FULL // tile
+            real, _, both, less = triple(turned[base:base + VECTORS], turned[base + VECTORS:base + 2 * VECTORS], 1)
+            source[member, spin, :, :FULL] = real
+            source[member, spin, :, FULL:2 * FULL] = less
+            source[member, spin, :, 2 * FULL:] = both
+
+
+WIDTH = 256
+
+
+def meson_columns(columns, sink, source, member, n):
+    found = []
+    for part in range(3):
+        left = jnp.concatenate(
+            [sink[member, columns[0, spin], :, part * FULL:(part + 1) * FULL] for spin in range(SPINS)], axis=0
+        )
+        start = part * FULL + n * WIDTH
+        right = jnp.concatenate(
+            [source[member, columns[1, spin], :, start:start + WIDTH] for spin in range(SPINS)], axis=0
+        )
+        found.append(product(left, right, ((1,), (0,))))
+    return found[0] - found[2], found[0] + found[1]
+
+
+def folded(tile):
+    return jnp.sum(tile.reshape(-1, 8, tile.shape[1]), axis=0)
+
+
+def slot_value(columns, sink, source, flipped):
     eye = (
-        lax.broadcasted_iota(jnp.int32, (tile, tile), 0) == lax.broadcasted_iota(jnp.int32, (tile, tile), 1)
-    ).astype(F32)
-    traces = []
-    for member in range(2):
-        for part in range(2):
-            total = jnp.zeros((tile, tile), F32)
-            for i in range(count):
-                total += eye * meson[member, i * tile:(i + 1) * tile, part * FULL + i * tile:part * FULL + (i + 1) * tile]
-            traces.append(jnp.sum(total))
-
-    def step(i, carry):
-        box_real, box_imaginary = carry
-        rows = pl.ds(pl.multiple_of(i * tile, tile), tile)
-        for j in range(count):
-            here = slice(j * tile, (j + 1) * tile)
-            first_real = meson[0, rows, here]
-            first_imaginary = meson[0, rows, FULL + j * tile:FULL + (j + 1) * tile]
-            second_real = meson[1, here, rows].T
-            second_imaginary = meson[1, here, pl.ds(pl.multiple_of(FULL + i * tile, tile), tile)].T
-            box_real += first_real * second_real - first_imaginary * second_imaginary
-            box_imaginary += first_real * second_imaginary + first_imaginary * second_real
-        return box_real, box_imaginary
-
-    zero = jnp.zeros((tile, tile), F32)
-    box_real, box_imaginary = lax.fori_loop(0, count, step, (zero, zero))
-    one_real, one_imaginary, two_real, two_imaginary = traces
+        lax.broadcasted_iota(jnp.int32, (WIDTH, WIDTH), 0) == lax.broadcasted_iota(jnp.int32, (WIDTH, WIDTH), 1)
+    )
+    zero = jnp.zeros((8, WIDTH), F32)
+    traces = [[zero, zero], [zero, zero]]
+    box_real = box_imaginary = zero
+    for member in (1, 0):
+        for n in range(FULL // WIDTH):
+            at = slice(n * WIDTH, (n + 1) * WIDTH)
+            parts = meson_columns(columns, sink, source, member, n)
+            for part in range(2):
+                traces[member][part] += folded(jnp.where(eye, parts[part][at], 0.0))
+            if member == 1:
+                for part in range(2):
+                    flipped[part, at, :] = parts[part].T
+            else:
+                real, imaginary = parts
+                box_real += folded(real * flipped[0, :, at] - imaginary * flipped[1, :, at])
+                box_imaginary += folded(real * flipped[1, :, at] + imaginary * flipped[0, :, at])
+    one_real, one_imaginary = (jnp.sum(part) for part in traces[0])
+    two_real, two_imaginary = (jnp.sum(part) for part in traces[1])
     direct_real = one_real * two_real - one_imaginary * two_imaginary
     direct_imaginary = one_real * two_imaginary + one_imaginary * two_real
     return (direct_real - jnp.sum(box_real)) * 0.0625, (direct_imaginary - jnp.sum(box_imaginary)) * 0.0625
@@ -190,7 +192,7 @@
 
 def correlator_kernel(
     order, times, columns, phases, group, peramb, elementals, out, staged_own, staged_far, picked, pieces, held, block,
-    sink_left, source_left, sink, source, meson, votes, load_sem, self_sem, send_plane, recv_plane, send_ring,
+    sink_left, source_left, sink, source, flipped, votes, load_sem, self_sem, send_plane, recv_plane, send_ring,
     recv_ring, send_core, recv_core, send_vote, recv_vote,
 ):
     x, z, y, core = place()
@@ -293,8 +295,7 @@
 
     gather_rows(pieces, block, x, z)
     sides(block, sink_left, source_left, sink, source)
-    mesons(columns, sink, source, meson)
-    real, imaginary = slot_value(meson)
+    real, imaginary = slot_value(columns, sink, source, flipped)
 
     row = lax.broadcasted_iota(jnp.int32, (8, 128), 0)
     lane = lax.broadcasted_iota(jnp.int32, (8, 128), 1)
@@ -339,9 +340,9 @@
             pltpu.VMEM((FULL, 2 * FULL), BF16),
             pltpu.VMEM((SPINS, 2, FULL, 256), BF16),
             pltpu.VMEM((SPINS, 2, FULL, 256), BF16),
-            pltpu.VMEM((2, SPINS, VECTORS, 2 * FULL), BF16),
-            pltpu.VMEM((2, 2, SPINS, VECTORS, 2 * FULL), BF16),
-            pltpu.VMEM((2, FULL, 2 * FULL), F32),
+            pltpu.VMEM((2, SPINS, VECTORS, 3 * FULL), BF16),
+            pltpu.VMEM((2, SPINS, VECTORS, 3 * FULL), BF16),
+            pltpu.VMEM((2, FULL, FULL), F32),
             pltpu.VMEM((2 * NY, 8, 128), F32),
             dma((3,)),
             dma((2,)),

time: 55.3 us -> 50 us (0.904)
  Pallas kernels: 53.3 us -> 48 us
    pallas_call x1, Pallas kernels: 53.3 us -> 48 us  [per_device(): pl.pallas_call(correlator_kernel, out_shape=jax.ShapeDtypeStruct((2, 1, G...]
where the time goes in v3:
time: 50 us; the launch traced here: 49.9 us
  Pallas kernels  48 us (96%)
  local copies, waits for them, and re-layouts  1.24 us (2%)
  between operations  0.66 us (1%)
    pallas_call x1, Pallas kernels, per_device(): pl.pallas_call(correlator_kernel, out_shape=jax.ShapeDtypeStruct((2, 1, G...  48 us
    unnamed x1, local copies, waits for them, and re-layouts  1.24 us

profile of v3, /device:TPU:1, one launch (start us, length us, event | category | flops | bytes accessed | tf_op | source)
XLA Modules:
  0.0 49.9 jit_solution(6976028175241940137)
XLA Ops:
  0.7 48.0 %correlator.1 = f32[2,1,8]{2,1,0:T(1,128)} custom-call(s32[32]{0:T(128)} %order.1, s32[2,32]{1,0:T(2,128)} %bitcast.1, s32[2,4]{1,0:T(2,128)} %columns.1, s32[2,4]{1,0:T(2,128)} %phases.1, s32[1]{0:T(128)S(6)} %copy.9.group, bf16[32,24,1536]{2,1,0:T(8,128)(2,1)} %peramb.1, bf16[16,1,2,192,384]{4,3,2,1,0:T(8,128)(2,1)} %elementals.1), custom_call_target="tpu_custom_call" | custom-call | flops 11000000512 | bytes 8000000 | tf_op jit(solution)/shard_map/correlator/pallas_call | solution.py:329
  48.6 1.2 %copy.10 = f32[2,1,8]{2,1,0:T(1,128)} copy(f32[2,1,8]{2,1,0:T(1,128)} %correlator.1) | data formatting | bytes 128

commit v4 on v3

--- a/solution.py
+++ b/solution.py
@@ -17,6 +17,8 @@
 ROWS = 24
 PIECE = 384
 PEERS = 16
+STEPS = 4
+EACH = PEERS // STEPS
 
 
 def place():
@@ -92,18 +94,17 @@
                 left[spin, 1, lower, :] = (-turned_real).astype(BF16)
 
 
-def gather_rows(pieces, block, x, z):
+def gather_rows(pieces, block, x, z, piece):
     def position(s):
         dx, dz = (x + NX - s // NZ) % NX, (z + NZ - s % NZ) % NZ
         return dz % 2, dx * 4 + dz // 2
 
     def step(i, carry):
         one, two = position(2 * i), position(2 * i + 1)
-        for piece in range(NY):
-            a = pieces[piece, one[0], one[1]].astype(F32)
-            b = pieces[piece, two[0], two[1]].astype(F32)
-            rows = pl.ds(pl.multiple_of(i * 2 * ROWS, 16), 2 * ROWS)
-            block[rows, piece * PIECE:(piece + 1) * PIECE] = jnp.concatenate([a, b], axis=0).astype(BF16)
+        a = pieces[piece, one[0], one[1]].astype(F32)
+        b = pieces[piece, two[0], two[1]].astype(F32)
+        rows = pl.ds(pl.multiple_of(i * 2 * ROWS, 16), 2 * ROWS)
+        block[rows, pl.ds(pl.multiple_of(piece * PIECE, 128), PIECE)] = jnp.concatenate([a, b], axis=0).astype(BF16)
         return carry
 
     lax.fori_loop(0, NX * NZ // 2, step, 0)
@@ -119,27 +120,64 @@
     return real, imaginary, (one + two).astype(BF16), None if sign == 0 else (two - one).astype(BF16)
 
 
-def sides(block, sink_left, source_left, sink, source):
+def lanes(start, width):
+    return pl.ds(pl.multiple_of(start, 128), width)
+
+
+def sink_part(block, sink_left, spin, step, part, piece):
+    here = block[:, lanes(piece * PIECE + step * 128, 256)]
+    return product(sink_left[spin, part], here, ((1,), (1,)))
+
+
+def source_part(block, source_left, spin, part, piece):
+    start = (spin // 2) * PIECE + (spin % 2) * 128
+    here = block[start:start + 256, lanes(piece * PIECE, PIECE)]
+    return product(source_left[spin, part], here, ((1,), (0,)))
+
+
+def member_parts(turned, member):
+    base = member * 2 * VECTORS
+    return turned[base:base + VECTORS], turned[base + VECTORS:base + 2 * VECTORS]
+
+
+def put_sink(sink, turned, spin):
+    for member in range(2):
+        real, imaginary, both, _ = triple(*member_parts(turned, member), 0)
+        sink[member, spin, :, :FULL] = both
+        sink[member, spin, :, FULL:2 * FULL] = real
+        sink[member, spin, :, 2 * FULL:] = imaginary
+
+
+def put_source(source, turned, spin, half):
+    for member in range(2):
+        real, _, both, less = triple(*member_parts(turned, member), 1)
+        for place_of, value in enumerate((real, less, both)):
+            source[member, spin, :, lanes(place_of * FULL + half * PIECE, PIECE)] = value
+
+
+def begin_sides(block, sink_left, source_left, sink_sum, source_sum, half, part, piece):
+    for step in range(2):
+        sink_sum[step] = sink_part(block, sink_left, 2 * half + step, step, part, piece)
     for spin in range(SPINS):
-        start = (spin // 2) * PIECE + (spin % 2) * 128
-        turned = product(sink_left[spin, 0], block[:, start:start + 256], ((1,), (1,)))
-        turned += product(sink_left[spin, 1], block[:, FULL + start:FULL + start + 256], ((1,), (1,)))
-        for member in range(2):
-            base = member * 2 * VECTORS
-            real, imaginary, both, _ = triple(turned[base:base + VECTORS], turned[base + VECTORS:base + 2 * VECTORS], 0)
-            sink[member, spin, :, :FULL] = both
-            sink[member, spin, :, FULL:2 * FULL] = real
-            sink[member, spin, :, 2 * FULL:] = imaginary
+        source_sum[spin] = source_part(block, source_left, spin, part, piece)
+
+
+def end_sides(block, sink_left, source_left, sink_sum, source_sum, sink, source, half, part, piece):
+    for step in range(2):
+        spin = 2 * half + step
+        put_sink(sink, sink_sum[step] + sink_part(block, sink_left, spin, step, part, piece), spin)
     for spin in range(SPINS):
-        start = (spin // 2) * PIECE + (spin % 2) * 128
-        turned = product(source_left[spin, 0], block[start:start + 256, :FULL], ((1,), (0,)))
-        turned += product(source_left[spin, 1], block[start:start + 256, FULL:], ((1,), (0,)))
-        for member in range(2):
-            base = member * 2 * VECTORS
-            real, _, both, less = triple(turned[base:base + VECTORS], turned[base + VECTORS:base + 2 * VECTORS], 1)
-            source[member, spin, :, :FULL] = real
-            source[member, spin, :, FULL:2 * FULL] = less
-            source[member, spin, :, 2 * FULL:] = both
+        put_source(source, source_sum[spin] + source_part(block, source_left, spin, part, piece), spin, half)
+
+
+def whole_sides(block, sink_left, source_left, sink, source, half):
+    for step in range(2):
+        spin = 2 * half + step
+        turned = sink_part(block, sink_left, spin, step, 0, half)
+        put_sink(sink, turned + sink_part(block, sink_left, spin, step, 1, half + 2), spin)
+    for spin in range(SPINS):
+        turned = source_part(block, source_left, spin, 0, half)
+        put_source(source, turned + source_part(block, source_left, spin, 1, half + 2), spin, half)
 
 
 WIDTH = 256
@@ -192,7 +230,7 @@
 
 def correlator_kernel(
     order, times, columns, phases, group, peramb, elementals, out, staged_own, staged_far, picked, pieces, held, block,
-    sink_left, source_left, sink, source, flipped, votes, load_sem, self_sem, send_plane, recv_plane, send_ring,
+    sink_left, source_left, sink, source, sink_sum, source_sum, flipped, votes, load_sem, self_sem, send_plane, recv_plane, send_ring,
     recv_ring, send_core, recv_core, send_vote, recv_vote,
 ):
     x, z, y, core = place()
@@ -228,25 +266,23 @@
         pl.semaphore_signal(barrier, inc=1, device_id=plane(source_of(0)), device_id_type=MESH)
     for step in range(1, 2 * NY):
         pl.semaphore_signal(barrier, inc=1, device_id=peer(step), device_id_type=MESH)
-    loads[0].wait()
-    pl.semaphore_wait(barrier, PEERS - 1 + 2 * NY - 1 + core)
-
     def pick(phase):
         for j in range(PEERS):
             picked[phase, j] = staged[phase][order[target(j)]]
 
-    def send_in_plane(phase, piece):
-        for j in range(PEERS):
+    def send_in_plane(phase, piece, g):
+        for j in range(g * EACH, (g + 1) * EACH):
             src, dst = picked.at[phase, j], pieces.at[piece, core, j]
+            sem = recv_plane.at[phase, g]
             if j == 0:
                 @pl.when(core == 0)
                 def _():
-                    pltpu.make_async_copy(src, dst, recv_plane.at[phase]).start()
+                    pltpu.make_async_copy(src, dst, sem).start()
                 @pl.when(core == 1)
                 def _():
-                    copy_to(src, dst, self_sem.at[phase], recv_plane.at[phase], plane(target(j))).start()
+                    copy_to(src, dst, self_sem.at[phase], sem, plane(target(j))).start()
             else:
-                copy_to(src, dst, send_plane.at[phase], recv_plane.at[phase], plane(target(j))).start()
+                copy_to(src, dst, send_plane.at[phase], sem, plane(target(j))).start()
 
     def sent_in_plane(phase):
         most = picked.at[phase, pl.ds(1, PEERS - 1)]
@@ -256,45 +292,66 @@
             one = picked.at[phase, 0]
             pltpu.make_async_copy(one, one, self_sem.at[phase]).wait()
 
-    def finish(piece, side, sem):
-        part = pieces.at[piece, side]
-        pltpu.make_async_copy(part, part, sem).wait()
-
-    def to_ring(way, where):
-        part = pieces.at[y, core]
-        copy_to(part, part, send_ring.at[way], recv_ring.at[way], column(where, core)).start()
-
-    def to_other(kind, piece):
-        part = pieces.at[piece, core]
-        copy_to(part, part, send_core.at[kind], recv_core.at[kind], column(y, other)).start()
-
+    def part(piece, side, g):
+        return pieces.at[piece, side, pl.ds(g * EACH, EACH)]
+
+    def finish(piece, side, sem, g):
+        here = part(piece, side, g)
+        pltpu.make_async_copy(here, here, sem).wait()
+
+    def to_ring(way, where, g):
+        here = part(y, core, g)
+        copy_to(here, here, send_ring.at[way, g], recv_ring.at[way, g], column(where, core)).start()
+
+    def to_other(kind, piece, g):
+        here = part(piece, core, g)
+        copy_to(here, here, send_core.at[kind, g], recv_core.at[kind, g], column(y, other)).start()
+
+    loads[0].wait()
     pick(0)
-    send_in_plane(0, y)
+    pl.semaphore_wait(barrier, PEERS - 1 + 2 * NY - 1 + core)
+    for g in range(STEPS):
+        send_in_plane(0, y, g)
     loads[1].wait()
     pick(1)
+    for g in range(STEPS):
+        send_in_plane(1, far, g)
     loads[2].wait()
     chosen = order[lax.axis_index("pair")]
     prepare_left(lambda member: held[times[0, chosen], 0, member], columns, phases, 0, sink_left)
     prepare_left(lambda member: held[times[1, chosen], 0, member], columns, phases, 1, source_left)
 
-    finish(y, core, recv_plane.at[0])
-    to_ring(0, up)
-    to_ring(1, down)
-    send_in_plane(1, far)
-    to_other(0, y)
-    finish(y, other, recv_core.at[0])
-    finish(down, core, recv_ring.at[0])
-    to_other(1, down)
-    finish(up, core, recv_ring.at[1])
-    to_other(2, up)
-    finish(far, core, recv_plane.at[1])
-    to_other(3, far)
-    finish(down, other, recv_core.at[1])
-    finish(up, other, recv_core.at[2])
-    finish(far, other, recv_core.at[3])
-
-    gather_rows(pieces, block, x, z)
-    sides(block, sink_left, source_left, sink, source)
+    for g in range(STEPS):
+        finish(y, core, recv_plane.at[0, g], g)
+        to_ring(0, up, g)
+        to_ring(1, down, g)
+        to_other(0, y, g)
+    half, part_of = y % 2, y // 2
+    for g in range(STEPS):
+        finish(y, other, recv_core.at[0, g], g)
+    gather_rows(pieces, block, x, z, y)
+    begin_sides(block, sink_left, source_left, sink_sum, source_sum, half, part_of, y)
+
+    for g in range(STEPS):
+        finish(down, core, recv_ring.at[0, g], g)
+        to_other(1, down, g)
+        finish(up, core, recv_ring.at[1, g], g)
+        to_other(2, up, g)
+    for g in range(STEPS):
+        finish(far, core, recv_plane.at[1, g], g)
+        to_other(3, far, g)
+    for g in range(STEPS):
+        finish(down, other, recv_core.at[1, g], g)
+        finish(up, other, recv_core.at[2, g], g)
+    gather_rows(pieces, block, x, z, down)
+    gather_rows(pieces, block, x, z, up)
+    whole_sides(block, sink_left, source_left, sink, source, 1 - half)
+
+    for g in range(STEPS):
+        finish(far, other, recv_core.at[3, g], g)
+    gather_rows(pieces, block, x, z, far)
+    end_sides(block, sink_left, source_left, sink_sum, source_sum, sink, source, half, 1 - part_of, far)
+
     real, imaginary = slot_value(columns, sink, source, flipped)
 
     row = lax.broadcasted_iota(jnp.int32, (8, 128), 0)
@@ -306,18 +363,18 @@
 
     sent_in_plane(0)
     sent_in_plane(1)
-    for way in range(2):
-        finish(y, core, send_ring.at[way])
-    for kind, piece in enumerate((y, down, up, far)):
-        finish(piece, core, send_core.at[kind])
+    for g in range(STEPS):
+        for way in range(2):
+            finish(y, core, send_ring.at[way, g], g)
+        for kind, piece in enumerate((y, down, up, far)):
+            finish(piece, core, send_core.at[kind, g], g)
     for step in range(1, 2 * NY):
         sender = (mom + 2 * NY - step) % (2 * NY)
         pltpu.make_async_copy(votes.at[sender], votes.at[sender], recv_vote.at[step]).wait()
     total = votes[0]
     for each in range(1, 2 * NY):
         total = total + votes[each]
-    out[0] = total[0:1, :GROUPS]
-    out[1] = total[1:2, :GROUPS]
+    out[...] = total
     for step in range(1, 2 * NY):
         pltpu.make_async_copy(votes.at[mom], votes.at[mom], send_vote.at[step]).wait()
 
@@ -326,9 +383,9 @@
     smem = pl.BlockSpec(memory_space=pltpu.SMEM)
     anywhere = pl.BlockSpec(memory_space=pl.ANY)
     dma = pltpu.SemaphoreType.DMA
-    return pl.pallas_call(
+    found = pl.pallas_call(
         correlator_kernel,
-        out_shape=jax.ShapeDtypeStruct((2, 1, GROUPS), F32),
+        out_shape=jax.ShapeDtypeStruct((8, 128), F32),
         in_specs=[smem] * 5 + [anywhere] * 2,
         out_specs=pl.BlockSpec(memory_space=pltpu.VMEM),
         scratch_shapes=[
@@ -343,15 +400,17 @@
             pltpu.VMEM((2, SPINS, VECTORS, 3 * FULL), BF16),
             pltpu.VMEM((2, SPINS, VECTORS, 3 * FULL), BF16),
             pltpu.VMEM((2, FULL, FULL), F32),
+            pltpu.VMEM((SPINS, FULL, PIECE), F32),
+            pltpu.VMEM((2, FULL, FULL), F32),
             pltpu.VMEM((2 * NY, 8, 128), F32),
             dma((3,)),
             dma((2,)),
             dma((2,)),
-            dma((2,)),
-            dma((2,)),
-            dma((2,)),
-            dma((4,)),
-            dma((4,)),
+            dma((2, STEPS)),
+            dma((2, STEPS)),
+            dma((2, STEPS)),
+            dma((4, STEPS)),
+            dma((4, STEPS)),
             dma((2 * NY,)),
             dma((2 * NY,)),
         ],
@@ -361,6 +420,7 @@
         cost_estimate=pl.CostEstimate(flops=11_000_000_000, bytes_accessed=8_000_000, transcendentals=0),
         name="correlator",
     )(pair_order, pair_times.T, gamma_columns, gamma_phases, class_group, peramb, elementals)
+    return found[:2, :GROUPS].reshape(2, 1, GROUPS)
 
 
 def solution(mesh):

time: 50 us -> 47 us (0.940)
  Pallas kernels: 48 us -> 45 us
    pallas_call x1, Pallas kernels: 48 us -> 45 us  [per_device(): pl.pallas_call(correlator_kernel, out_shape=jax.ShapeDtypeStruct((8, 128)...]
    slice x0 -> x1, local copies, waits for them, and re-layouts: none -> 1.25 us  [per_device(): return found[:2, :GROUPS].reshape(2, 1, GROUPS)]
    unnamed x1 -> x0, local copies, waits for them, and re-layouts: 1.24 us -> none
where the time goes in v4:
time: 47 us; the launch traced here: 46.9 us
  Pallas kernels  45 us (96%)
  local copies, waits for them, and re-layouts  1.25 us (3%)
  between operations  0.66 us (1%)
    pallas_call x1, Pallas kernels, per_device(): pl.pallas_call(correlator_kernel, out_shape=jax.ShapeDtypeStruct((8, 128)...  45 us
    slice x1, local copies, waits for them, and re-layouts, per_device(): return found[:2, :GROUPS].reshape(2, 1, GROUPS)  1.25 us

profile of v4, /device:TPU:1, one launch (start us, length us, event | category | flops | bytes accessed | tf_op | source)
XLA Modules:
  0.0 46.9 jit_solution(15463835302948344251)
XLA Ops:
  0.7 45.0 %correlator.1 = f32[8,128]{1,0:T(8,128)} custom-call(s32[32]{0:T(128)} %order.1, s32[2,32]{1,0:T(2,128)} %bitcast.4, s32[2,4]{1,0:T(2,128)} %columns.1, s32[2,4]{1,0:T(2,128)} %phases.1, s32[1]{0:T(128)S(6)} %copy.9.group, bf16[32,24,1536]{2,1,0:T(8,128)(2,1)} %peramb.1, bf16[16,1,2,192,384]{4,3,2,1,0:T(8,128)(2,1)} %elementals.1), custom_call_target="tpu_custom_call" | custom-call | flops 11000000512 | bytes 8000000 | tf_op jit(solution)/shard_map/correlator/pallas_call | solution.py:386
  45.6 1.2 %slice.3 = f32[2,8]{1,0:T(2,128)} slice(f32[8,128]{1,0:T(8,128)} %correlator.1), slice={[0:2], [0:8]} | slice | bytes 128 | tf_op jit(solution)/shard_map/slice | solution.py:423

commit v5 on v4

--- a/solution.py
+++ b/solution.py
@@ -19,6 +19,10 @@
 PEERS = 16
 STEPS = 4
 EACH = PEERS // STEPS
+OFFSETS = (
+    (0, 0), (0, 3), (1, 0), (3, 0), (0, 1), (1, 3), (3, 3), (2, 0),
+    (0, 2), (1, 1), (3, 1), (2, 3), (1, 2), (3, 2), (2, 1), (2, 2),
+)
 
 
 def place():
@@ -95,19 +99,16 @@
 
 
 def gather_rows(pieces, block, x, z, piece):
-    def position(s):
-        dx, dz = (x + NX - s // NZ) % NX, (z + NZ - s % NZ) % NZ
-        return dz % 2, dx * 4 + dz // 2
-
-    def step(i, carry):
-        one, two = position(2 * i), position(2 * i + 1)
-        a = pieces[piece, one[0], one[1]].astype(F32)
-        b = pieces[piece, two[0], two[1]].astype(F32)
-        rows = pl.ds(pl.multiple_of(i * 2 * ROWS, 16), 2 * ROWS)
-        block[rows, pl.ds(pl.multiple_of(piece * PIECE, 128), PIECE)] = jnp.concatenate([a, b], axis=0).astype(BF16)
-        return carry
-
-    lax.fori_loop(0, NX * NZ // 2, step, 0)
+    odd = z % 2
+    for dx in range(NX):
+        for v in range(4):
+            first = OFFSETS.index((dx, v))
+            second = jnp.where(odd == 1, first, OFFSETS.index((dx, (v + 3) % 4)))
+            pair = ((x + NX - dx) % NX) * NZ + (z + NZ - 2 * v - odd) % NZ
+            a = pieces[piece, odd, first].astype(F32)
+            b = pieces[piece, 1 - odd, second].astype(F32)
+            rows = pl.ds(pl.multiple_of(pair * ROWS, 16), 2 * ROWS)
+            block[rows, pl.ds(pl.multiple_of(piece * PIECE, 128), PIECE)] = jnp.concatenate([a, b], axis=0).astype(BF16)
 
 
 def product(left, right, dims):
@@ -127,12 +128,6 @@
 def sink_part(block, sink_left, spin, step, part, piece):
     here = block[:, lanes(piece * PIECE + step * 128, 256)]
     return product(sink_left[spin, part], here, ((1,), (1,)))
-
-
-def source_part(block, source_left, spin, part, piece):
-    start = (spin // 2) * PIECE + (spin % 2) * 128
-    here = block[start:start + 256, lanes(piece * PIECE, PIECE)]
-    return product(source_left[spin, part], here, ((1,), (0,)))
 
 
 def member_parts(turned, member):
@@ -148,36 +143,34 @@
         sink[member, spin, :, 2 * FULL:] = imaginary
 
 
-def put_source(source, turned, spin, half):
-    for member in range(2):
-        real, _, both, less = triple(*member_parts(turned, member), 1)
-        for place_of, value in enumerate((real, less, both)):
-            source[member, spin, :, lanes(place_of * FULL + half * PIECE, PIECE)] = value
-
-
-def begin_sides(block, sink_left, source_left, sink_sum, source_sum, half, part, piece):
+def begin_sink(block, sink_left, sink_sum, half, part, piece):
     for step in range(2):
         sink_sum[step] = sink_part(block, sink_left, 2 * half + step, step, part, piece)
-    for spin in range(SPINS):
-        source_sum[spin] = source_part(block, source_left, spin, part, piece)
-
-
-def end_sides(block, sink_left, source_left, sink_sum, source_sum, sink, source, half, part, piece):
+
+
+def end_sink(block, sink_left, sink_sum, sink, half, part, piece):
     for step in range(2):
         spin = 2 * half + step
         put_sink(sink, sink_sum[step] + sink_part(block, sink_left, spin, step, part, piece), spin)
-    for spin in range(SPINS):
-        put_source(source, source_sum[spin] + source_part(block, source_left, spin, part, piece), spin, half)
-
-
-def whole_sides(block, sink_left, source_left, sink, source, half):
+
+
+def whole_sink(block, sink_left, sink, half):
     for step in range(2):
         spin = 2 * half + step
         turned = sink_part(block, sink_left, spin, step, 0, half)
         put_sink(sink, turned + sink_part(block, sink_left, spin, step, 1, half + 2), spin)
+
+
+def whole_source(block, source_left, source):
     for spin in range(SPINS):
-        turned = source_part(block, source_left, spin, 0, half)
-        put_source(source, turned + source_part(block, source_left, spin, 1, half + 2), spin, half)
+        start = (spin // 2) * PIECE + (spin % 2) * 128
+        turned = product(source_left[spin, 0], block[start:start + 256, :FULL], ((1,), (0,)))
+        turned += product(source_left[spin, 1], block[start:start + 256, FULL:], ((1,), (0,)))
+        for member in range(2):
+            real, _, both, less = triple(*member_parts(turned, member), 1)
+            source[member, spin, :, :FULL] = real
+            source[member, spin, :, FULL:2 * FULL] = less
+            source[member, spin, :, 2 * FULL:] = both
 
 
 WIDTH = 256
@@ -230,7 +223,7 @@
 
 def correlator_kernel(
     order, times, columns, phases, group, peramb, elementals, out, staged_own, staged_far, picked, pieces, held, block,
-    sink_left, source_left, sink, source, sink_sum, source_sum, flipped, votes, load_sem, self_sem, send_plane, recv_plane, send_ring,
+    sink_left, source_left, sink, source, sink_sum, flipped, votes, load_sem, self_sem, send_plane, recv_plane, send_ring,
     recv_ring, send_core, recv_core, send_vote, recv_vote,
 ):
     x, z, y, core = place()
@@ -239,11 +232,11 @@
     other = 1 - core
 
     def target(j):
-        dx, dz = j // 4, 2 * (j % 4) + core
+        dx, dz = OFFSETS[j][0], 2 * OFFSETS[j][1] + core
         return ((x + dx) % NX) * NZ + (z + dz) % NZ
 
     def source_of(j):
-        dx, dz = j // 4, 2 * (j % 4) + core
+        dx, dz = OFFSETS[j][0], 2 * OFFSETS[j][1] + core
         return ((x + NX - dx) % NX) * NZ + (z + NZ - dz) % NZ
 
     def peer(step):
@@ -330,7 +323,7 @@
     for g in range(STEPS):
         finish(y, other, recv_core.at[0, g], g)
     gather_rows(pieces, block, x, z, y)
-    begin_sides(block, sink_left, source_left, sink_sum, source_sum, half, part_of, y)
+    begin_sink(block, sink_left, sink_sum, half, part_of, y)
 
     for g in range(STEPS):
         finish(down, core, recv_ring.at[0, g], g)
@@ -345,12 +338,13 @@
         finish(up, other, recv_core.at[2, g], g)
     gather_rows(pieces, block, x, z, down)
     gather_rows(pieces, block, x, z, up)
-    whole_sides(block, sink_left, source_left, sink, source, 1 - half)
+    whole_sink(block, sink_left, sink, 1 - half)
 
     for g in range(STEPS):
         finish(far, other, recv_core.at[3, g], g)
     gather_rows(pieces, block, x, z, far)
-    end_sides(block, sink_left, source_left, sink_sum, source_sum, sink, source, half, 1 - part_of, far)
+    end_sink(block, sink_left, sink_sum, sink, half, 1 - part_of, far)
+    whole_source(block, source_left, source)
 
     real, imaginary = slot_value(columns, sink, source, flipped)
 
@@ -400,7 +394,6 @@
             pltpu.VMEM((2, SPINS, VECTORS, 3 * FULL), BF16),
             pltpu.VMEM((2, SPINS, VECTORS, 3 * FULL), BF16),
             pltpu.VMEM((2, FULL, FULL), F32),
-            pltpu.VMEM((SPINS, FULL, PIECE), F32),
             pltpu.VMEM((2, FULL, FULL), F32),
             pltpu.VMEM((2 * NY, 8, 128), F32),
             dma((3,)),

time: 47 us -> 45.4 us (0.966)
  Pallas kernels: 45 us -> 43.3 us
    pallas_call x1, Pallas kernels: 45 us -> 43.3 us  [per_device(): pl.pallas_call(correlator_kernel, out_shape=jax.ShapeDtypeStruct((8, 128)...]
where the time goes in v5:
time: 45.4 us; the launch traced here: 45.2 us
  Pallas kernels  43.3 us (95%)
  local copies, waits for them, and re-layouts  1.25 us (3%)
  between operations  0.66 us (1%)
    pallas_call x1, Pallas kernels, per_device(): pl.pallas_call(correlator_kernel, out_shape=jax.ShapeDtypeStruct((8, 128)...  43.3 us
    slice x1, local copies, waits for them, and re-layouts, per_device(): return found[:2, :GROUPS].reshape(2, 1, GROUPS)  1.25 us

profile of v5, /device:TPU:1, one launch (start us, length us, event | category | flops | bytes accessed | tf_op | source)
XLA Modules:
  0.0 45.2 jit_solution(6448567796828547935)
XLA Ops:
  0.7 43.3 %correlator.1 = f32[8,128]{1,0:T(8,128)} custom-call(s32[32]{0:T(128)} %order.1, s32[2,32]{1,0:T(2,128)} %bitcast.4, s32[2,4]{1,0:T(2,128)} %columns.1, s32[2,4]{1,0:T(2,128)} %phases.1, s32[1]{0:T(128)S(6)} %copy.9.group, bf16[32,24,1536]{2,1,0:T(8,128)(2,1)} %peramb.1, bf16[16,1,2,192,384]{4,3,2,1,0:T(8,128)(2,1)} %elementals.1), custom_call_target="tpu_custom_call" | custom-call | flops 11000000512 | bytes 8000000 | tf_op jit(solution)/shard_map/correlator/pallas_call | solution.py:380
  44.0 1.2 %slice.3 = f32[2,8]{1,0:T(2,128)} slice(f32[8,128]{1,0:T(8,128)} %correlator.1), slice={[0:2], [0:8]} | slice | bytes 128 | tf_op jit(solution)/shard_map/slice | solution.py:416

commit v6 on v5

--- a/solution.py
+++ b/solution.py
@@ -307,8 +307,6 @@
         send_in_plane(0, y, g)
     loads[1].wait()
     pick(1)
-    for g in range(STEPS):
-        send_in_plane(1, far, g)
     loads[2].wait()
     chosen = order[lax.axis_index("pair")]
     prepare_left(lambda member: held[times[0, chosen], 0, member], columns, phases, 0, sink_left)
@@ -318,6 +316,9 @@
         finish(y, core, recv_plane.at[0, g], g)
         to_ring(0, up, g)
         to_ring(1, down, g)
+        if g == 0:
+            for later in range(STEPS):
+                send_in_plane(1, far, later)
         to_other(0, y, g)
     half, part_of = y % 2, y // 2
     for g in range(STEPS):

time: 45.4 us -> 45.7 us (level)
  no operation moved by 1% of the time
where the time goes in v6:
time: 45.7 us; the launch traced here: 45.5 us
  Pallas kernels  43.6 us (95%)
  local copies, waits for them, and re-layouts  1.25 us (3%)
  between operations  0.66 us (1%)
    pallas_call x1, Pallas kernels, per_device(): pl.pallas_call(correlator_kernel, out_shape=jax.ShapeDtypeStruct((8, 128)...  43.6 us
    slice x1, local copies, waits for them, and re-layouts, per_device(): return found[:2, :GROUPS].reshape(2, 1, GROUPS)  1.25 us

profile of v6, /device:TPU:1, one launch (start us, length us, event | category | flops | bytes accessed | tf_op | source)
XLA Modules:
  0.0 45.5 jit_solution(15360068693261618655)
XLA Ops:
  0.7 43.6 %correlator.1 = f32[8,128]{1,0:T(8,128)} custom-call(s32[32]{0:T(128)} %order.1, s32[2,32]{1,0:T(2,128)} %bitcast.4, s32[2,4]{1,0:T(2,128)} %columns.1, s32[2,4]{1,0:T(2,128)} %phases.1, s32[1]{0:T(128)S(6)} %copy.9.group, bf16[32,24,1536]{2,1,0:T(8,128)(2,1)} %peramb.1, bf16[16,1,2,192,384]{4,3,2,1,0:T(8,128)(2,1)} %elementals.1), custom_call_target="tpu_custom_call" | custom-call | flops 11000000512 | bytes 8000000 | tf_op jit(solution)/shard_map/correlator/pallas_call | solution.py:381
  44.3 1.2 %slice.3 = f32[2,8]{1,0:T(2,128)} slice(f32[8,128]{1,0:T(8,128)} %correlator.1), slice={[0:2], [0:8]} | slice | bytes 128 | tf_op jit(solution)/shard_map/slice | solution.py:417
